TPU v7x, 32 devices: a whole 2x2x4 slice. The times are simulated.
32 devices in a mesh: row: 16 (over z, y, x), col: 2 (over core).
Axes of the slice: x: 2, y: 2, z: 4, core: 2. Of those that a mesh axis runs over, the one named last changes fastest.
Arguments:
- object_field: float32 [2, 4096, 512], P(None, 'row', 'col'), may hold values from -6 to 6
- probe_field: float32 [2, 256, 256], replicated, may hold values from -6 to 6
- amplitudes: float32 [32, 512, 256], P('row', 'col'), may hold values from 0 to 4
- offsets: int32 [16, 2, 2, 2], P('row', 'col'), may hold values from 0 to 128, as said below
- counts: int32 [16, 2], P('row', 'col'), may hold values from 1 to 2
Outputs:
- object_out: float32 [2, 4096, 512], P(None, 'row', 'col')
- probe_out: float32 [2, 256, 256], replicated
Inputs may be any that keep to these rules, and one draw needn't show every extreme that they name: `offsets`: slots from counts[r, c] on are padding and hold no window.
All inputs are finite; a program needn't handle non-finite values.
Results may differ from a plain program's by a relative error of at most 0.0003.
Values sent between devices are 32-bit elements; how exact they have to be, the bound alone decides.
A program may use at most 64 MiB of HBM per device.

v0:
```python
import functools
import math

import jax
import jax.numpy as jnp
import numpy as np
from jax import lax
from jax.experimental import pallas as pl
from jax.experimental.pallas import tpu as pltpu
from jax.sharding import PartitionSpec as P

HALO = 128
OUTER = 2


smooth_floor = 0.5
object_step = 0.5
tiny_value = 1e-06


def shifted(value, axis, by):
    length = lax.axis_size(axis)
    pairs = [(i, i + by) for i in range(length) if 0 <= i + by < length]
    return lax.ppermute(value, axis, pairs)


def make_tables(length):
    half = length // 2
    first = np.arange(half)[:, None]
    second = np.arange(half)[None, :]
    tables = []
    for parity in range(2):
        angles = (first * (2 * second + parity) % length) * (-2.0 * math.pi / length)
        real = np.cos(angles) / math.sqrt(length)
        imag = np.sin(angles) / math.sqrt(length)
        tables.append(np.block([[real, imag], [-imag, real]]))
    tables += [tables[0].T, tables[1].T]
    stacked = np.stack(tables).astype(np.float32)
    upper = stacked.astype(jnp.bfloat16)
    lower = (stacked - upper.astype(np.float32)).astype(jnp.bfloat16)
    sorting = np.zeros((length, length), np.float32)
    sorting[np.arange(length), np.arange(length) // 2 + half * (np.arange(length) % 2)] = 1.0
    return np.concatenate([upper, lower, sorting.astype(jnp.bfloat16)[None]])


def split(value):
    upper = value.astype(jnp.bfloat16)
    lower = (value - upper.astype(jnp.float32)).astype(jnp.bfloat16)
    return upper, lower


def dot(left, right):
    return jnp.dot(left, right, preferred_element_type=jnp.float32)


def times_table(value, tables, index):
    upper, lower = split(value)
    return (
        dot(upper, tables[index]) + dot(lower, tables[index]) + dot(upper, tables[index + 4])
    )


def table_times(tables, index, value):
    upper, lower = split(value)
    return (
        dot(tables[index], upper) + dot(tables[index], lower) + dot(tables[index + 4], upper)
    )


def lanes(*parts):
    return jnp.concatenate(parts, axis=1)


def stack(*parts):
    return jnp.concatenate(parts, axis=0)


def halves_of_lanes(value):
    half = value.shape[1] // 2
    return value[:, :half], value[:, half:]


def halves_of_rows(value):
    half = value.shape[0] // 2
    return value[:half], value[half:]


def forward(real, imag, tables):
    real_l, real_r = halves_of_lanes(real)
    imag_l, imag_r = halves_of_lanes(imag)
    even = times_table(lanes(real_l + real_r, imag_l + imag_r), tables, 0)
    odd = times_table(lanes(real_l - real_r, imag_l - imag_r), tables, 1)
    even_t, even_b = halves_of_rows(even)
    odd_t, odd_b = halves_of_rows(odd)
    even_re, even_im = halves_of_lanes(even_t + even_b)
    odd_re, odd_im = halves_of_lanes(odd_t + odd_b)
    top = table_times(tables, 2, stack(lanes(even_re, odd_re), lanes(even_im, odd_im)))
    even_re, even_im = halves_of_lanes(even_t - even_b)
    odd_re, odd_im = halves_of_lanes(odd_t - odd_b)
    bottom = table_times(tables, 3, stack(lanes(even_re, odd_re), lanes(even_im, odd_im)))
    return top, bottom


def inverse(top, bottom, tables):
    top = table_times(tables, 0, top)
    bottom = table_times(tables, 1, bottom)
    upper_re, upper_im = halves_of_rows(top + bottom)
    lower_re, lower_im = halves_of_rows(top - bottom)
    even_ur, odd_ur = halves_of_lanes(upper_re)
    even_ui, odd_ui = halves_of_lanes(upper_im)
    even_lr, odd_lr = halves_of_lanes(lower_re)
    even_li, odd_li = halves_of_lanes(lower_im)
    even = times_table(stack(lanes(even_ur, even_ui), lanes(even_lr, even_li)), tables, 2)
    odd = times_table(stack(lanes(odd_ur, odd_ui), lanes(odd_lr, odd_li)), tables, 3)
    left_re, left_im = halves_of_lanes(even + odd)
    right_re, right_im = halves_of_lanes(even - odd)
    return lanes(left_re, right_re), lanes(left_im, right_im)


def sorted_amplitudes(amp_ref, slot, tables, hold):
    upper, lower = split(amp_ref[slot])
    value = dot(upper, tables[8]) + dot(lower, tables[8])
    left, right = halves_of_lanes(value)
    hold[0] = left
    hold[1] = right
    half = value.shape[0] // 2
    return [
        lanes(
            hold[0, pl.ds(parity, half, stride=2), :], hold[1, pl.ds(parity, half, stride=2), :]
        )
        for parity in range(2)
    ]


def cut_window(slabs, part, first_row, first_col, window, margin):
    lane = lax.broadcasted_iota(jnp.int32, (window, margin), 1)
    inside = lane < margin - first_col
    turn = lax.rem(margin - first_col, margin)
    turned = [
        pltpu.roll(slabs[part, slab, pl.ds(first_row, window), :], turn, 1)
        for slab in range(slabs.shape[1])
    ]
    return lanes(*[jnp.where(inside, a, b) for a, b in zip(turned[:-1], turned[1:])])


def place_lanes(term, first_col, margin):
    window = term.shape[0]
    lane = lax.broadcasted_iota(jnp.int32, (window, margin), 1)
    inside = lane >= first_col
    turn = lax.rem(first_col, margin)
    turned = [
        pltpu.roll(term[:, at : at + margin], turn, 1) for at in range(0, term.shape[1], margin)
    ]
    empty = jnp.zeros((window, margin), term.dtype)
    return [jnp.where(inside, a, b) for a, b in zip(turned + [empty], [empty] + turned)]


def pass_over_windows(
    off_ref, cnt_ref, ext_ref, probe_ref, amp_ref, tables, grad_ref, pgrad_ref, hold, slabs, padded
):
    slot_count = amp_ref.shape[0]
    window = probe_ref.shape[1]
    ext_rows = ext_ref.shape[1]
    margin = ext_rows - window
    for part in range(2):
        for slab in range(slabs.shape[1]):
            slabs[part, slab] = ext_ref[part, :, slab * margin : (slab + 1) * margin]
    probe_re = probe_ref[0]
    probe_im = probe_ref[1]
    power = None
    for slot in range(slot_count):
        first_row = off_ref[0, 0, slot, 0]
        first_col = off_ref[0, 0, slot, 1]
        live = (slot < cnt_ref[0, 0]).astype(jnp.float32)
        win_re = cut_window(slabs, 0, first_row, first_col, window, margin)
        win_im = cut_window(slabs, 1, first_row, first_col, window, margin)
        spectrum = forward(
            probe_re * win_re - probe_im * win_im, probe_re * win_im + probe_im * win_re, tables
        )
        replaced = []
        for hat, measured in zip(spectrum, sorted_amplitudes(amp_ref, slot, tables, hold.at[slot])):
            hat_re, hat_im = halves_of_rows(hat)
            ratio = measured * lax.rsqrt(hat_re * hat_re + hat_im * hat_im + smooth_floor) - 1.0
            ratio = ratio * live
            replaced.append(stack(hat_re * ratio, hat_im * ratio))
        diff_re, diff_im = inverse(*replaced, tables)
        terms = (probe_re * diff_re + probe_im * diff_im, probe_re * diff_im - probe_im * diff_re)
        for part, term in enumerate(terms):
            empty = jnp.zeros((margin, margin), jnp.float32)
            for slab, placed in enumerate(place_lanes(term, first_col, margin)):
                box = padded.at[slot, part, slab]
                box[:margin] = empty
                box[margin : margin + window] = placed
                box[margin + window :] = empty
                shown = box[pl.ds(margin - first_row, ext_rows), :]
                here = slice(slab * margin, (slab + 1) * margin)
                if slot == 0:
                    grad_ref[part, :, here] = shown
                else:
                    grad_ref[part, :, here] += shown
        probe_terms = (win_re * diff_re + win_im * diff_im, win_re * diff_im - win_im * diff_re)
        for part, term in enumerate(probe_terms):
            pgrad_ref[part] = term if slot == 0 else pgrad_ref[part] + term
        squares = jnp.sum(win_re * win_re + win_im * win_im, axis=0, keepdims=True) * live
        power = squares if power is None else power + squares
    return power


def pass_kernel(
    off_ref, cnt_ref, ext_ref, probe_ref, amp_ref, tables, grad_ref, pgrad_ref, power_ref, *scratch
):
    power = pass_over_windows(
        off_ref, cnt_ref, ext_ref, probe_ref, amp_ref, tables, grad_ref, pgrad_ref, *scratch
    )
    power_ref[...] = jnp.broadcast_to(power, power_ref.shape)


def one_pass(extended, probe, amplitudes, offsets, counts, tables):
    slots, window = amplitudes.shape[0], probe.shape[1]
    ext_rows, ext_cols = extended.shape[1:]
    margin = ext_rows - window
    smem = pl.BlockSpec(memory_space=pltpu.SMEM)
    vmem = pl.BlockSpec(memory_space=pltpu.VMEM)
    return pl.pallas_call(
        pass_kernel,
        out_shape=(
            jax.ShapeDtypeStruct(extended.shape, jnp.float32),
            jax.ShapeDtypeStruct(probe.shape, jnp.float32),
            jax.ShapeDtypeStruct((8, window), jnp.float32),
        ),
        in_specs=[smem, smem, vmem, vmem, vmem, vmem],
        out_specs=(vmem, vmem, vmem),
        scratch_shapes=[
            pltpu.VMEM((slots, 2, window, window // 2), jnp.float32),
            pltpu.VMEM((2, ext_cols // margin, ext_rows, margin), jnp.float32),
            pltpu.VMEM((slots, 2, ext_cols // margin, window + 2 * margin, margin), jnp.float32),
        ],
        compiler_params=pltpu.CompilerParams(vmem_limit_bytes=40 * 2**20),
        name="window_pass",
    )(offsets, counts, extended, probe, amplitudes, tables)


def shards(object_field, probe_field, amplitudes, offsets, counts):
    tile_rows = object_field.shape[1]
    tile_cols = object_field.shape[2]
    window = probe_field.shape[1]
    margin = HALO
    tables = jnp.asarray(make_tables(window))
    current = object_field
    probe_now = probe_field
    for outer_step in range(OUTER):
        probe_mean = jnp.sum(probe_now * probe_now) / (window * window)
        lower_rows = shifted(current[:, :margin, :], "row", -1)
        taller = jnp.concatenate([current, lower_rows], axis=1)
        right_cols = shifted(taller[:, :, :margin], "col", -1)
        extended = jnp.concatenate([taller, right_cols], axis=2)
        grad_ext, probe_grad, power = one_pass(
            extended, probe_now, amplitudes, offsets, counts, tables
        )
        rim_right = shifted(grad_ext[:, :, tile_cols:], "col", 1)
        narrowed = grad_ext[:, :, :tile_cols]
        narrowed = jnp.concatenate(
            [narrowed[:, :, :margin] + rim_right, narrowed[:, :, margin:]], axis=2
        )
        rim_lower = shifted(narrowed[:, tile_rows:, :], "row", 1)
        tile_grad = jnp.concatenate(
            [narrowed[:, :margin, :] + rim_lower, narrowed[:, margin:tile_rows, :]], axis=1
        )
        current = current + object_step * tile_grad / (probe_mean + tiny_value)
        power_old = jnp.sum(probe_now * probe_now)
        summed_grad, summed_power = lax.psum((probe_grad, power[0]), ("row", "col"))
        moved_probe = probe_now + summed_grad / (
            jnp.sum(summed_power) / (window * window) + tiny_value
        )
        power_new = jnp.sum(moved_probe * moved_probe)
        probe_now = moved_probe * jnp.sqrt(power_old / (power_new + tiny_value))
    return (current, probe_now)


def solution(mesh):
    return jax.shard_map(
        shards,
        mesh=mesh,
        in_specs=(
            P(None, "row", "col"),
            P(),
            P("row", "col", None),
            P("row", "col", None, None),
            P("row", "col"),
        ),
        out_specs=(P(None, "row", "col"), P()),
        check_vma=False,
    )
```

profile of v0, /device:TPU:25, one launch (start us, length us, event | category | flops | bytes accessed | tf_op | source)
XLA Modules:
  0.0 334.3 jit_solution(7837232337106910381)
XLA Ops:
  8.2 4.0 %collective-permute-start = (f32[2,128,256]{2,1,0:T(8,128)S(1)}, f32[2,128,256]{2,1,0:T(8,128)S(1)}, u32[]{:S(2)}, u32[]{:S(2)}) collective-permute-start(f32[2,128,256]{2,1,0:T(8,128)S(1)} %slice.60), channel_id=1, source_target_pairs={{2,0},{4,2},{6,4},{8,6},{10,8},{12,10},{14,12},{16,14},{18,16},{20... | collective-permute-start | bytes 786440 | tf_op jit(solution)/shard_map/ppermute | solution.py:24
  13.2 4.0 %collective-permute-done = f32[2,128,256]{2,1,0:T(8,128)S(1)} collective-permute-done((f32[2,128,256]{2,1,0:T(8,128)S(1)}, f32[2,128,256]{2,1,0:T(8,128)S(1)}, u32[]{:S(2)}, u32[]{:S(2)}) %collective-permute-start) | collective-permute-done | bytes 262176 | tf_op jit(solution)/shard_map/ppermute | solution.py:24
  17.3 3.5 %collective-permute-start.1 = (f32[2,384,128]{2,1,0:T(8,128)S(1)}, f32[2,384,128]{2,1,0:T(8,128)S(1)}, u32[]{:S(2)}, u32[]{:S(2)}) collective-permute-start(f32[2,384,128]{2,1,0:T(8,128)S(1)} %slice.78), channel_id=1, source_target_pairs={{1,0},{3,2},{5,4},{7,6},{9,8},{11,10},{13,12},{15,14},{17,16},{19,... | collective-permute-start | bytes 1179656 | tf_op jit(solution)/shard_map/ppermute | solution.py:24
  23.0 4.5 %window_pass.2 = (f32[2,384,384]{2,1,0:T(8,128)S(1)}, f32[2,256,256]{2,1,0:T(8,128)S(1)}, f32[8,256]{1,0:T(8,128)S(1)}) custom-call(s32[1,1,2,2]{3,2,1,0:T(2,128)S(1)} %copy-done.6, s32[1,1]{1,0:T(1,128)S(6)} %copy.11.cnt_ref, f32[2,384,384]{2,1,0:T(8,128)S(1)} %pad_maximum_fusion.ext_ref, f32[2,256,256]{2,1,0:T(8,128)S(1)} %copy-done.1, ...), custom_call_target="tpu_custom_call" | custom-call | tf_op jit(solution)/shard_map/window_pass/pallas_call | solution.py:224
  29.0 1.3 collective-permute-start.2
  30.4 2.6 collective-permute-done.2
  34.9 4.0 %collective-permute-start.3 = (f32[2,128,256]{2,1,0:T(8,128)}, f32[2,128,256]{2,1,0:T(8,128)S(1)}, u32[]{:S(2)}, u32[]{:S(2)}) collective-permute-start(f32[2,128,256]{2,1,0:T(8,128)} %fusion.11), channel_id=1, source_target_pairs={{0,2},{2,4},{4,6},{6,8},{8,10},{10,12},{12,14},{14,16},{16,18},{18... | collective-permute-start | bytes 786440 | tf_op jit(solution)/shard_map/ppermute | solution.py:24
  38.9 39.9 %psum.29 = f32[256]{0:T(256)S(1)} all-reduce(f32[256]{0:T(256)S(1)} %bitcast.2), channel_id=1, replica_groups=mesh['row'=16,'col'=2] {'row','col'}, use_global_device_ids=true, to_apply=%region_2.0 | all-reduce | flops 256 | bytes 2048 | tf_op jit(solution)/shard_map/psum | solution.py:271
  80.2 78.6 %all-reduce.3.cloned.1.call-done = f32[2,256,256]{2,1,0:T(8,128)} async-done(((f32[2,256,256]{2,1,0:T(8,128)}), f32[2,256,256]{2,1,0:T(8,128)}) %all-reduce.3.cloned.1.call-update) | async-done | bytes 524304 | tf_op jit(solution)/shard_map/psum | solution.py:271
  158.8 1.9 multiply_reduce_fusion.2
  161.3 1.2 fusion.7
  162.5 3.4 %collective-permute-start.4 = (f32[2,128,256]{2,1,0:T(8,128)S(1)}, f32[2,128,256]{2,1,0:T(8,128)S(1)}, u32[]{:S(2)}, u32[]{:S(2)}) collective-permute-start(f32[2,128,256]{2,1,0:T(8,128)S(1)} %slice.83), channel_id=1, source_target_pairs={{2,0},{4,2},{6,4},{8,6},{10,8},{12,10},{14,12},{16,14},{18,16},{20... | collective-permute-start | bytes 786440 | tf_op jit(solution)/shard_map/ppermute | solution.py:24
  166.0 3.7 %collective-permute-done.4 = f32[2,128,256]{2,1,0:T(8,128)S(1)} collective-permute-done((f32[2,128,256]{2,1,0:T(8,128)S(1)}, f32[2,128,256]{2,1,0:T(8,128)S(1)}, u32[]{:S(2)}, u32[]{:S(2)}) %collective-permute-start.4) | collective-permute-done | bytes 262176 | tf_op jit(solution)/shard_map/ppermute | solution.py:24
  170.4 6.1 %collective-permute-start.5 = (f32[2,384,128]{2,1,0:T(8,128)}, f32[2,384,128]{2,1,0:T(8,128)}, u32[]{:S(2)}, u32[]{:S(2)}) collective-permute-start(f32[2,384,128]{2,1,0:T(8,128)} %pad_maximum_fusion.2), channel_id=1, source_target_pairs={{1,0},{3,2},{5,4},{7,6},{9,8},{11,10},{13,12},{15,14},{17,16},{19,... | collective-permute-start | bytes 1179656 | tf_op jit(solution)/shard_map/ppermute | solution.py:24
  177.9 1.2 broadcast_multiply_fusion.1.probe_ref
  180.2 4.9 %window_pass.3 = (f32[2,384,384]{2,1,0:T(8,128)S(1)}, f32[2,256,256]{2,1,0:T(8,128)}, f32[8,256]{1,0:T(8,128)S(1)}) custom-call(s32[1,1,2,2]{3,2,1,0:T(2,128)S(1)} %copy-done.6, s32[1,1]{1,0:T(1,128)S(6)} %copy.11.cnt_ref, f32[2,384,384]{2,1,0:T(8,128)S(1)} %pad_maximum_fusion.1.ext_ref, f32[2,256,256]{2,1,0:T(8,128)S(1)} %broadcast_multiply_fusion.1.probe_ref, ...), custom_call_target="tpu_custom_call" | custom-call | tf_op jit(solution)/shard_map/window_pass/pallas_call | solution.py:224
  186.2 1.1 slice.72
  187.3 1.3 collective-permute-start.6
  188.6 42.2 %psum.31 = f32[256]{0:T(256)S(1)} all-reduce(f32[256]{0:T(256)S(1)} %bitcast.3), channel_id=1, replica_groups=mesh['row'=16,'col'=2] {'row','col'}, use_global_device_ids=true, to_apply=%region_7.0 | all-reduce | flops 256 | bytes 2048 | tf_op jit(solution)/shard_map/psum | solution.py:271
  232.0 80.7 %all-reduce.5.cloned.1.call-done = f32[2,256,256]{2,1,0:T(8,128)} async-done(((f32[2,256,256]{2,1,0:T(8,128)}), f32[2,256,256]{2,1,0:T(8,128)}) %all-reduce.5.cloned.1.call-update) | async-done | bytes 524304 | tf_op jit(solution)/shard_map/psum | solution.py:271
  312.7 1.8 multiply_reduce_fusion
  316.5 1.1 slice_add_fusion
  317.7 3.1 collective-permute-start.7
  321.6 4.9 %collective-permute-done.7 = f32[2,128,256]{2,1,0:T(8,128)S(1)} collective-permute-done((f32[2,128,256]{2,1,0:T(8,128)S(1)}, f32[2,128,256]{2,1,0:T(8,128)S(1)}, u32[]{:S(2)}, u32[]{:S(2)}) %collective-permute-start.7) | collective-permute-done | bytes 262176 | tf_op jit(solution)/shard_map/ppermute | solution.py:24
  (56 shorter events, 13.2 us)
Async XLA Ops:
  7.2 151.6 %all-reduce.3.cloned.1.call-start = ((), (), s32[]{:S(2)}) async-start(), calls=%async_computation | async-start | bytes 1048576 | tf_op jit(solution)/shard_map/psum | solution.py:271
  8.2 9.1 %collective-permute-start = (f32[2,128,256]{2,1,0:T(8,128)S(1)}, f32[2,128,256]{2,1,0:T(8,128)S(1)}, u32[]{:S(2)}, u32[]{:S(2)}) collective-permute-start(f32[2,128,256]{2,1,0:T(8,128)S(1)} %slice.60), channel_id=1, source_target_pairs={{2,0},{4,2},{6,4},{8,6},{10,8},{12,10},{14,12},{16,14},{18,16},{20... | collective-permute-start | bytes 786440 | tf_op jit(solution)/shard_map/ppermute | solution.py:24
  17.3 4.8 %collective-permute-start.1 = (f32[2,384,128]{2,1,0:T(8,128)S(1)}, f32[2,384,128]{2,1,0:T(8,128)S(1)}, u32[]{:S(2)}, u32[]{:S(2)}) collective-permute-start(f32[2,384,128]{2,1,0:T(8,128)S(1)} %slice.78), channel_id=1, source_target_pairs={{1,0},{3,2},{5,4},{7,6},{9,8},{11,10},{13,12},{15,14},{17,16},{19,... | collective-permute-start | bytes 1179656 | tf_op jit(solution)/shard_map/ppermute | solution.py:24
  21.4 1.3 copy-start
  21.5 1.4 copy-start.1
  21.5 1.5 copy-start.2
  21.5 1.5 copy-start.6
  27.5 0.8 copy-start.5
  29.0 3.9 %collective-permute-start.2 = (f32[2,384,128]{2,1,0:T(8,128)}, f32[2,384,128]{2,1,0:T(8,128)}, u32[]{:S(2)}, u32[]{:S(2)}) collective-permute-start(f32[2,384,128]{2,1,0:T(8,128)} %slice.63), channel_id=1, source_target_pairs={{0,1},{2,3},{4,5},{6,7},{8,9},{10,11},{12,13},{14,15},{16,17},{18,... | collective-permute-start | bytes 1179656 | tf_op jit(solution)/shard_map/ppermute | solution.py:24
  30.4 282.4 %all-reduce.5.cloned.1.call-start = ((), (), s32[]{:S(2)}) async-start(), calls=%async_computation.1 | async-start | bytes 1048576 | tf_op jit(solution)/shard_map/psum | solution.py:271
  34.1 4.8 %copy-start.7 = (f32[2,384,128]{2,1,0:T(8,128)}, f32[2,384,128]{2,1,0:T(8,128)S(1)}, u32[]{:S(2)}) copy-start(f32[2,384,128]{2,1,0:T(8,128)S(1)} %get-tuple-element.20) | copy-start | bytes 1179652
  34.1 4.8 %copy-start.9 = (f32[2,384,128]{2,1,0:T(8,128)}, f32[2,384,128]{2,1,0:T(8,128)S(1)}, u32[]{:S(2)}) copy-start(f32[2,384,128]{2,1,0:T(8,128)S(1)} %get-tuple-element.21) | copy-start | bytes 1179652
  34.9 126.4 %collective-permute-start.3 = (f32[2,128,256]{2,1,0:T(8,128)}, f32[2,128,256]{2,1,0:T(8,128)S(1)}, u32[]{:S(2)}, u32[]{:S(2)}) collective-permute-start(f32[2,128,256]{2,1,0:T(8,128)} %fusion.11), channel_id=1, source_target_pairs={{0,2},{2,4},{4,6},{6,8},{8,10},{10,12},{12,14},{14,16},{16,18},{18... | collective-permute-start | bytes 786440 | tf_op jit(solution)/shard_map/ppermute | solution.py:24
  38.9 122.3 %copy-start.8 = (f32[2,384,128]{2,1,0:T(8,128)S(1)}, f32[2,384,128]{2,1,0:T(8,128)}, u32[]{:S(2)}) copy-start(f32[2,384,128]{2,1,0:T(8,128)} %copy-done.7) | copy-start | bytes 1179652
  38.9 122.3 %copy-start.10 = (f32[2,384,128]{2,1,0:T(8,128)S(1)}, f32[2,384,128]{2,1,0:T(8,128)}, u32[]{:S(2)}) copy-start(f32[2,384,128]{2,1,0:T(8,128)} %copy-done.9) | copy-start | bytes 1179652
  162.5 7.1 %collective-permute-start.4 = (f32[2,128,256]{2,1,0:T(8,128)S(1)}, f32[2,128,256]{2,1,0:T(8,128)S(1)}, u32[]{:S(2)}, u32[]{:S(2)}) collective-permute-start(f32[2,128,256]{2,1,0:T(8,128)S(1)} %slice.83), channel_id=1, source_target_pairs={{2,0},{4,2},{6,4},{8,6},{10,8},{12,10},{14,12},{16,14},{18,16},{20... | collective-permute-start | bytes 786440 | tf_op jit(solution)/shard_map/ppermute | solution.py:24
  169.6 8.2 %copy-start.12 = (f32[2,128,256]{2,1,0:T(8,128)}, f32[2,128,256]{2,1,0:T(8,128)S(1)}, u32[]{:S(2)}) copy-start(f32[2,128,256]{2,1,0:T(8,128)S(1)} %collective-permute-done.4) | copy-start | bytes 786436
  170.4 8.6 %collective-permute-start.5 = (f32[2,384,128]{2,1,0:T(8,128)}, f32[2,384,128]{2,1,0:T(8,128)}, u32[]{:S(2)}, u32[]{:S(2)}) collective-permute-start(f32[2,384,128]{2,1,0:T(8,128)} %pad_maximum_fusion.2), channel_id=1, source_target_pairs={{1,0},{3,2},{5,4},{7,6},{9,8},{11,10},{13,12},{15,14},{17,16},{19,... | collective-permute-start | bytes 1179656 | tf_op jit(solution)/shard_map/ppermute | solution.py:24
  177.9 1.2 copy-start.13
  185.1 1.0 copy-start.3
  186.1 130.4 %copy-start.4 = (f32[2,384,384]{2,1,0:T(8,128)S(1)}, f32[2,384,384]{2,1,0:T(8,128)}, u32[]{:S(2)}) copy-start(f32[2,384,384]{2,1,0:T(8,128)} %copy-done.3) | copy-start | bytes 3538948
  187.3 129.2 %collective-permute-start.6 = (f32[2,384,128]{2,1,0:T(8,128)S(1)}, f32[2,384,128]{2,1,0:T(8,128)}, u32[]{:S(2)}, u32[]{:S(2)}) collective-permute-start(f32[2,384,128]{2,1,0:T(8,128)S(1)} %slice.72), channel_id=1, source_target_pairs={{0,1},{2,3},{4,5},{6,7},{8,9},{10,11},{12,13},{14,15},{16,17},{18,... | collective-permute-start | bytes 1179656 | tf_op jit(solution)/shard_map/ppermute | solution.py:24
  316.5 4.3 %copy-start.11 = (f32[2,256,256]{2,1,0:T(8,128)S(1)}, f32[2,256,256]{2,1,0:T(8,128)}, u32[]{:S(2)}) copy-start(f32[2,256,256]{2,1,0:T(8,128)} %all-reduce.5.cloned.1.call-done) | copy-start | bytes 1572868
  317.7 8.9 %collective-permute-start.7 = (f32[2,128,256]{2,1,0:T(8,128)S(1)}, f32[2,128,256]{2,1,0:T(8,128)S(1)}, u32[]{:S(2)}, u32[]{:S(2)}) collective-permute-start(f32[2,128,256]{2,1,0:T(8,128)S(1)} %fusion.8), channel_id=1, source_target_pairs={{0,2},{2,4},{4,6},{6,8},{8,10},{10,12},{12,14},{14,16},{16,18},{18... | collective-permute-start | bytes 786440 | tf_op jit(solution)/shard_map/ppermute | solution.py:24
Sparse Core Ops, SparseCore 0:
  30.5 128.2 all-reduce.2
  186.3 126.3 all-reduce.4
where the time goes:
time: 339 us; the launch traced here: 334 us
  waiting for transfers between devices  175 us (52%)
  blocking collectives  82 us (24%)
  starting transfers between devices  26.8 us (8%)
  between operations  20.2 us (6%)
  other arithmetic  14 us (4%)
  Pallas kernels  9.39 us (3%)
  local copies, waits for them, and re-layouts  6.69 us (2%)
    psum x2, waiting for transfers between devices, shards(): summed_grad, summed_power = lax.psum((probe_grad, power[0]), ('row', 'col'))  159 us
    psum x2, blocking collectives, shards(): summed_grad, summed_power = lax.psum((probe_grad, power[0]), ('row', 'col'))  82 us
    ppermute x8, starting transfers between devices, shifted(): return lax.ppermute(value, axis, pairs)  26.7 us
    ppermute x8, waiting for transfers between devices, shifted(): return lax.ppermute(value, axis, pairs)  15.8 us
    pallas_call x2, Pallas kernels, one_pass(): pl.pallas_call(pass_kernel, out_shape=(jax.ShapeDtypeStruct(extended.shap...  9.39 us
  transfers between devices with their start and end apart: 10, of which 7 were waited for; matrix products, arithmetic and copies ran while one was open for 3% of the time, Pallas kernels for 0%

commit v1 on v0

--- a/solution.py
+++ b/solution.py
@@ -9,6 +9,7 @@
 from jax.experimental.pallas import tpu as pltpu
 from jax.sharding import PartitionSpec as P
 
+MESH = pl.DeviceIdType.MESH
 HALO = 128
 OUTER = 2
 
@@ -240,6 +241,496 @@
     )(offsets, counts, extended, probe, amplitudes, tables)
 
 
+def remote(src, dst, send_sem, recv_sem, **where):
+    return pltpu.make_async_remote_copy(
+        src_ref=src,
+        dst_ref=dst,
+        send_sem=send_sem,
+        recv_sem=recv_sem,
+        device_id=where,
+        device_id_type=MESH,
+    )
+
+
+class Place:
+    def __init__(self):
+        self.rows = lax.axis_size("row")
+        self.cols = lax.axis_size("col")
+        self.row = lax.axis_index("row")
+        self.col = lax.axis_index("col")
+        self.has_up = self.row > 0
+        self.has_down = self.row < self.rows - 1
+        self.has_left = self.col > 0
+        self.has_right = self.col < self.cols - 1
+        self.up = lax.max(self.row - 1, 0)
+        self.down = lax.min(self.row + 1, self.rows - 1)
+        self.left = lax.max(self.col - 1, 0)
+        self.right = lax.min(self.col + 1, self.cols - 1)
+
+    def other_row(self, step):
+        return lax.rem(self.row + step, self.rows)
+
+    def other_col(self, step):
+        return lax.rem(self.col + step, self.cols)
+
+    def greet(self):
+        barrier = pltpu.get_barrier_semaphore()
+        for step in range(1, self.cols):
+            pl.semaphore_signal(
+                barrier, inc=1, device_id={"col": self.other_col(step)}, device_id_type=MESH
+            )
+        for step in range(1, self.rows):
+            pl.semaphore_signal(
+                barrier, inc=1, device_id={"row": self.other_row(step)}, device_id_type=MESH
+            )
+
+    def await_greetings(self):
+        pl.semaphore_wait(pltpu.get_barrier_semaphore(), self.rows + self.cols - 2)
+
+
+class Halo:
+    @staticmethod
+    def scratch(tile_rows, tile_cols, margin):
+        return [
+            pltpu.VMEM((2, margin, tile_cols), jnp.float32),
+            pltpu.VMEM((2, tile_rows, margin), jnp.float32),
+            pltpu.VMEM((2, margin, margin), jnp.float32),
+            pltpu.SemaphoreType.DMA((3,)),
+            pltpu.SemaphoreType.DMA((3,)),
+        ]
+
+    def __init__(self, place, object_ref, below, beside, corner, sent, came):
+        self.place, self.object_ref = place, object_ref
+        self.below, self.beside, self.corner = below, beside, corner
+        margin = corner.shape[1]
+        self.margin = margin
+        self.from_below = remote(
+            object_ref.at[:, pl.ds(0, margin), :], below, sent.at[0], came.at[0], row=place.up
+        )
+        self.from_beside = remote(
+            object_ref.at[:, :, pl.ds(0, margin)], beside, sent.at[1], came.at[1], col=place.left
+        )
+        self.from_corner = remote(
+            below.at[:, :, pl.ds(0, margin)], corner, sent.at[2], came.at[2], col=place.left
+        )
+
+    def start(self):
+        pl.when(self.place.has_up)(self.from_below.start)
+        pl.when(self.place.has_left)(self.from_beside.start)
+
+    def finish(self, ext_ref):
+        place, margin = self.place, self.margin
+        _, tile_rows, tile_cols = self.object_ref.shape
+        ext_ref[:, :tile_rows, :tile_cols] = self.object_ref[...]
+
+        @pl.when(place.has_down)
+        def _():
+            self.from_below.wait_recv()
+            pl.when(place.has_left)(self.from_corner.start)
+            ext_ref[:, tile_rows:, :tile_cols] = self.below[...]
+
+        @pl.when(jnp.logical_not(place.has_down))
+        def _():
+            ext_ref[:, tile_rows:, :] = jnp.zeros((2, margin, tile_cols + margin), jnp.float32)
+
+        @pl.when(place.has_right)
+        def _():
+            self.from_beside.wait_recv()
+            ext_ref[:, :tile_rows, tile_cols:] = self.beside[...]
+
+            @pl.when(place.has_down)
+            def _():
+                self.from_corner.wait_recv()
+                ext_ref[:, tile_rows:, tile_cols:] = self.corner[...]
+
+        @pl.when(jnp.logical_not(place.has_right))
+        def _():
+            ext_ref[:, :, tile_cols:] = jnp.zeros((2, tile_rows + margin, margin), jnp.float32)
+
+    def settle(self):
+        place = self.place
+        pl.when(place.has_up)(self.from_below.wait_send)
+        pl.when(place.has_left)(self.from_beside.wait_send)
+        pl.when(jnp.logical_and(place.has_left, place.has_down))(self.from_corner.wait_send)
+
+
+class Rims:
+    @staticmethod
+    def scratch(tile_rows, tile_cols, margin):
+        tall, wide = tile_rows + margin, tile_cols + margin
+        return [
+            pltpu.VMEM((2, tall, wide), jnp.float32),
+            pltpu.VMEM((2, tall, margin), jnp.float32),
+            pltpu.VMEM((2, tall, margin), jnp.float32),
+            pltpu.VMEM((2, margin, tile_cols), jnp.float32),
+            pltpu.VMEM((2, margin, tile_cols), jnp.float32),
+            pltpu.VMEM((2, margin, margin), jnp.float32),
+            pltpu.VMEM((2, margin, margin), jnp.float32),
+            pltpu.SemaphoreType.DMA((6,)),
+            pltpu.SemaphoreType.DMA((6,)),
+        ]
+
+    def __init__(self, place, last, grad, total, left, right, above, below, over, under, sent, came):
+        self.place, self.last, self.grad, self.total = place, last, grad, total
+        self.left, self.right, self.above, self.below = left, right, above, below
+        self.over, self.under = over, under
+        margin = over.shape[1]
+        tile_rows, tile_cols = grad.shape[1] - margin, grad.shape[2] - margin
+        self.sizes = margin, tile_rows, tile_cols
+        first, own = pl.ds(0, margin), pl.ds(0, tile_cols)
+        self.to_right = remote(
+            grad.at[:, :, pl.ds(tile_cols, margin)], left, sent.at[0], came.at[0], col=place.right
+        )
+        self.to_left = remote(grad.at[:, :, first], right, sent.at[1], came.at[1], col=place.left)
+        self.to_down = remote(
+            total.at[:, pl.ds(tile_rows, margin), own], above, sent.at[2], came.at[2], row=place.down
+        )
+        self.to_up = remote(total.at[:, first, own], below, sent.at[3], came.at[3], row=place.up)
+        self.pass_over = remote(
+            above.at[:, :, first], over, sent.at[4], came.at[4], col=place.left
+        )
+        self.pass_under = remote(
+            below.at[:, :, first], under, sent.at[5], came.at[5], col=place.left
+        )
+
+    def start(self):
+        pl.when(self.place.has_right)(self.to_right.start)
+        if not self.last:
+            pl.when(self.place.has_left)(self.to_left.start)
+
+    def start_rows(self):
+        place, grad, total = self.place, self.grad, self.total
+        margin, tile_rows, tile_cols = self.sizes
+        total[...] = grad[...]
+
+        @pl.when(place.has_left)
+        def _():
+            self.to_right.wait_recv()
+            total[:, :, :margin] += self.left[...]
+
+        if not self.last:
+
+            @pl.when(place.has_right)
+            def _():
+                self.to_left.wait_recv()
+                total[:, :, tile_cols:] += self.right[...]
+
+        pl.when(place.has_down)(self.to_down.start)
+        if not self.last:
+            pl.when(place.has_up)(self.to_up.start)
+
+    def finish(self, old_ref, new_ref, factor):
+        place, total = self.place, self.total
+        margin, tile_rows, tile_cols = self.sizes
+        new_ref[:, margin:tile_rows, :tile_cols] = (
+            old_ref[:, margin:tile_rows, :tile_cols] + factor * total[:, margin:tile_rows, :tile_cols]
+        )
+
+        @pl.when(place.has_up)
+        def _():
+            self.to_down.wait_recv()
+            if not self.last:
+                pl.when(place.has_left)(self.pass_over.start)
+            new_ref[:, :margin, :tile_cols] = old_ref[:, :margin, :tile_cols] + factor * (
+                total[:, :margin, :tile_cols] + self.above[...]
+            )
+
+        @pl.when(jnp.logical_not(place.has_up))
+        def _():
+            new_ref[:, :margin, :tile_cols] = (
+                old_ref[:, :margin, :tile_cols] + factor * total[:, :margin, :tile_cols]
+            )
+
+        if self.last:
+            return
+
+        @pl.when(place.has_down)
+        def _():
+            self.to_up.wait_recv()
+            pl.when(place.has_left)(self.pass_under.start)
+            new_ref[:, tile_rows:, :tile_cols] = old_ref[:, tile_rows:, :tile_cols] + factor * (
+                total[:, tile_rows:, :tile_cols] + self.below[...]
+            )
+
+        @pl.when(jnp.logical_not(place.has_down))
+        def _():
+            new_ref[:, tile_rows:, :] = jnp.zeros((2, margin, tile_cols + margin), jnp.float32)
+
+        @pl.when(place.has_right)
+        def _():
+            new_ref[:, margin:tile_rows, tile_cols:] = (
+                old_ref[:, margin:tile_rows, tile_cols:]
+                + factor * total[:, margin:tile_rows, tile_cols:]
+            )
+
+            @pl.when(place.has_up)
+            def _():
+                self.pass_over.wait_recv()
+                new_ref[:, :margin, tile_cols:] = old_ref[:, :margin, tile_cols:] + factor * (
+                    total[:, :margin, tile_cols:] + self.over[...]
+                )
+
+            @pl.when(jnp.logical_not(place.has_up))
+            def _():
+                new_ref[:, :margin, tile_cols:] = (
+                    old_ref[:, :margin, tile_cols:] + factor * total[:, :margin, tile_cols:]
+                )
+
+            @pl.when(place.has_down)
+            def _():
+                self.pass_under.wait_recv()
+                new_ref[:, tile_rows:, tile_cols:] = old_ref[:, tile_rows:, tile_cols:] + factor * (
+                    total[:, tile_rows:, tile_cols:] + self.under[...]
+                )
+
+        @pl.when(jnp.logical_not(place.has_right))
+        def _():
+            new_ref[:, :, tile_cols:] = jnp.zeros((2, tile_rows + margin, margin), jnp.float32)
+
+    def settle(self):
+        place = self.place
+        pl.when(place.has_right)(self.to_right.wait_send)
+        pl.when(place.has_down)(self.to_down.wait_send)
+        if not self.last:
+            pl.when(place.has_left)(self.to_left.wait_send)
+            pl.when(place.has_up)(self.to_up.wait_send)
+            pl.when(jnp.logical_and(place.has_left, place.has_up))(self.pass_over.wait_send)
+            pl.when(jnp.logical_and(place.has_left, place.has_down))(self.pass_under.wait_send)
+
+
+class Sums:
+    extra = 8
+
+    @staticmethod
+    def chunk(rows, cols, window):
+        return 2 * window * window // 128 // (rows * cols)
+
+    @classmethod
+    def scratch(cls, rows, cols, window):
+        deep = cls.chunk(rows, cols, window)
+        full = deep + cls.extra
+        more_cols, more_rows = max(cols - 1, 1), rows - 1
+        return [
+            pltpu.VMEM((cols, rows, full, 128), jnp.float32),
+            pltpu.VMEM((more_cols, rows, full, 128), jnp.float32),
+            pltpu.VMEM((rows, full, 128), jnp.float32),
+            pltpu.VMEM((more_rows, full, 128), jnp.float32),
+            pltpu.VMEM((cols, rows, deep, 128), jnp.float32),
+            pltpu.SemaphoreType.DMA((2, more_cols)),
+            pltpu.SemaphoreType.DMA((2, more_rows)),
+            pltpu.SemaphoreType.DMA((2, more_rows)),
+            pltpu.SemaphoreType.DMA((2, more_cols, rows)),
+        ]
+
+    def __init__(self, place, whole, from_cols, part, from_rows, gathered, sems, sems2, sems3, sems4):
+        self.place, self.whole, self.from_cols, self.part = place, whole, from_cols, part
+        self.from_rows, self.gathered = from_rows, gathered
+        self.deep = gathered.shape[2]
+        self.over_cols = [
+            remote(
+                whole.at[place.other_col(step)],
+                from_cols.at[step - 1],
+                sems.at[0, step - 1],
+                sems.at[1, step - 1],
+                col=place.other_col(step),
+            )
+            for step in range(1, place.cols)
+        ]
+        self.over_rows = [
+            remote(
+                part.at[place.other_row(step)],
+                from_rows.at[step - 1],
+                sems2.at[0, step - 1],
+                sems2.at[1, step - 1],
+                row=place.other_row(step),
+            )
+            for step in range(1, place.rows)
+        ]
+        mine = gathered.at[place.col, place.row]
+        self.back_rows = [
+            remote(
+                mine,
+                mine,
+                sems3.at[0, step - 1],
+                sems3.at[1, step - 1],
+                row=place.other_row(step),
+            )
+            for step in range(1, place.rows)
+        ]
+        self.back_cols = []
+        for step in range(place.rows):
+            chunk = gathered.at[place.col, place.other_row(place.rows - step)]
+            self.back_cols.append(
+                [
+                    remote(
+                        chunk,
+                        chunk,
+                        sems4.at[0, other - 1, step],
+                        sems4.at[1, other - 1, step],
+                        col=place.other_col(other),
+                    )
+                    for other in range(1, place.cols)
+                ]
+            )
+
+    def slots(self, window):
+        per = window // self.deep
+        for number in range(self.place.cols * self.place.rows):
+            slab, at = divmod(number, per)
+            half, col = divmod(slab, window // 128)
+            yield half, col * 128, at * self.deep, number // self.place.rows, number % self.place.rows
+
+    def fill(self, pgrad_ref, power):
+        window = pgrad_ref.shape[1]
+        for half, lane, line, col, row in self.slots(window):
+            self.whole[col, row, : self.deep] = pgrad_ref[
+                half, line : line + self.deep, lane : lane + 128
+            ]
+        folded = sum(power[:, at : at + 128] for at in range(0, window, 128))
+        first = lax.broadcasted_iota(jnp.int32, (self.extra, 128), 0) == 0
+        block = jnp.where(first, jnp.broadcast_to(folded, (self.extra, 128)), 0.0)
+        for col in range(self.place.cols):
+            for row in range(self.place.rows):
+                self.whole[col, row, self.deep :] = block
+
+    def start(self):
+        for copy in self.over_cols:
+            copy.start()
+
+    def start_rows(self):
+        self.part[...] = self.whole[self.place.col]
+        for step, copy in enumerate(self.over_cols):
+            copy.wait_recv()
+            self.part[...] += self.from_cols[step]
+        for copy in self.over_rows:
+            copy.start()
+
+    def start_back(self):
+        total = self.part[self.place.row]
+        for step, copy in enumerate(self.over_rows):
+            copy.wait_recv()
+            total = total + self.from_rows[step]
+        self.gathered[self.place.col, self.place.row] = total[: self.deep]
+        for copy in self.back_rows + self.back_cols[0]:
+            copy.start()
+        return jnp.sum(total[self.deep :])
+
+    def pass_on(self):
+        for step, copy in enumerate(self.back_rows):
+            copy.wait_recv()
+            for other in self.back_cols[step + 1]:
+                other.start()
+
+    def finish(self, power, probe_ref, new_ref):
+        window = probe_ref.shape[1]
+        for copies in self.back_cols:
+            for copy in copies:
+                copy.wait_recv()
+        old = jnp.sum(probe_ref[...] * probe_ref[...], keepdims=True)
+        scale = 1.0 / (power / (window * window) + tiny_value)
+        for half, lane, line, col, row in self.slots(window):
+            here = (half, slice(line, line + self.deep), slice(lane, lane + 128))
+            moved = probe_ref[here] + self.gathered[col, row] * scale
+            new_ref[here] = moved
+        moved = new_ref[...]
+        new = jnp.sum(moved * moved, keepdims=True)
+        new_ref[...] = moved * jnp.sqrt(old / (new + tiny_value))
+
+    def settle(self):
+        for copy in self.over_cols + self.over_rows + self.back_rows:
+            copy.wait_send()
+        for copies in self.back_cols:
+            for copy in copies:
+                copy.wait_send()
+
+
+def halo_kernel(object_ref, ext_ref, *scratch):
+    place = Place()
+    place.greet()
+    halo = Halo(place, object_ref, *scratch)
+    place.await_greetings()
+    halo.start()
+    halo.finish(ext_ref)
+    halo.settle()
+
+
+def exchange_kernel(
+    rim_scratch, last, grad_ref, pgrad_ref, power_ref, ext_ref, probe_ref, out_ref, new_ref, *scratch
+):
+    place = Place()
+    place.greet()
+    rims = Rims(place, last, grad_ref, *scratch[:rim_scratch])
+    sums = Sums(place, *scratch[rim_scratch:])
+    sums.fill(pgrad_ref, power_ref[0:1])
+    place.await_greetings()
+    exchange(rims, sums, ext_ref, probe_ref, out_ref, new_ref)
+
+
+def exchange(rims, sums, ext_ref, probe_ref, out_ref, new_ref):
+    window = probe_ref.shape[1]
+    sums.start()
+    rims.start()
+    sums.start_rows()
+    rims.start_rows()
+    power = sums.start_back()
+    mean = jnp.sum(probe_ref[...] * probe_ref[...]) / (window * window)
+    rims.finish(ext_ref, out_ref, object_step / (mean + tiny_value))
+    sums.pass_on()
+    sums.finish(power, probe_ref, new_ref)
+    rims.settle()
+    sums.settle()
+
+
+def kernel_params(number):
+    return pltpu.CompilerParams(
+        collective_id=number, has_side_effects=True, vmem_limit_bytes=40 * 2**20
+    )
+
+
+def begin(object_field, margin):
+    _, tile_rows, tile_cols = object_field.shape
+    vmem = pl.BlockSpec(memory_space=pltpu.VMEM)
+    return pl.pallas_call(
+        halo_kernel,
+        out_shape=jax.ShapeDtypeStruct((2, tile_rows + margin, tile_cols + margin), jnp.float32),
+        in_specs=[vmem],
+        out_specs=vmem,
+        scratch_shapes=Halo.scratch(tile_rows, tile_cols, margin),
+        compiler_params=kernel_params(0),
+        name="first_halo",
+    )(object_field)
+
+
+def exchanged(last, margin, grad_ext, probe_grad, power, extended, probe):
+    tile_rows, tile_cols = extended.shape[1] - margin, extended.shape[2] - margin
+    rows, cols, window = lax.axis_size("row"), lax.axis_size("col"), probe.shape[1]
+    vmem = pl.BlockSpec(memory_space=pltpu.VMEM)
+    rim_scratch = Rims.scratch(tile_rows, tile_cols, margin)
+    out = (2, tile_rows, tile_cols) if last else extended.shape
+    return pl.pallas_call(
+        functools.partial(exchange_kernel, len(rim_scratch), last),
+        out_shape=(
+            jax.ShapeDtypeStruct(out, jnp.float32),
+            jax.ShapeDtypeStruct(probe.shape, jnp.float32),
+        ),
+        in_specs=[vmem] * 5,
+        out_specs=(vmem, vmem),
+        scratch_shapes=rim_scratch + Sums.scratch(rows, cols, window),
+        compiler_params=kernel_params(2 if last else 1),
+        name="last_exchange" if last else "exchange",
+    )(grad_ext, probe_grad, power, extended, probe)
+
+
+def shards_by_kernels(object_field, probe_field, amplitudes, offsets, counts):
+    tables = jnp.asarray(make_tables(probe_field.shape[1]))
+    extended = begin(object_field, HALO)
+    probe = probe_field
+    for outer_step in range(OUTER):
+        terms = one_pass(extended, probe, amplitudes, offsets, counts, tables)
+        extended, probe = exchanged(outer_step == OUTER - 1, HALO, *terms, extended, probe)
+    return (extended, probe)
+
+
 def shards(object_field, probe_field, amplitudes, offsets, counts):
     tile_rows = object_field.shape[1]
     tile_cols = object_field.shape[2]
@@ -278,8 +769,14 @@
 
 
 def solution(mesh):
+    rows, cols = mesh.shape["row"], mesh.shape["col"]
+
+    def shards_here(*args):
+        deep = Sums.chunk(rows, cols, args[1].shape[1])
+        return (shards_by_kernels if deep and deep % 8 == 0 else shards)(*args)
+
     return jax.shard_map(
-        shards,
+        shards_here,
         mesh=mesh,
         in_specs=(
             P(None, "row", "col"),

time: 339 us -> 81.1 us (0.24); the launches traced: 334 us -> 80.9 us
  waiting for transfers between devices: 175 us -> 0 us
  blocking collectives: 82 us -> 0 us
  Pallas kernels: 9.39 us -> 75.7 us
  starting transfers between devices: 26.8 us -> 0 us
  between operations: 20.2 us -> 1.51 us
  other arithmetic: 14 us -> 0 us
    psum x2 -> x0, waiting for transfers between devices: 159 us -> none  [shards(): summed_grad, summed_power = lax.psum((probe_grad, power[0]), ('row', 'col'))]
    psum x2 -> x0, blocking collectives: 82 us -> none  [shards(): summed_grad, summed_power = lax.psum((probe_grad, power[0]), ('row', 'col'))]
    pallas_call x0 -> x3, Pallas kernels: none -> 66.5 us  [the longest x2 57.3 us: exchanged(): pl.pallas_call(functools.partial(exchange_kernel, len(rim_scratch), last)...]
    ppermute x8 -> x0, starting transfers between devices: 26.7 us -> none  [shifted(): return lax.ppermute(value, axis, pairs)]
    ppermute x8 -> x0, waiting for transfers between devices: 15.8 us -> none  [shifted(): return lax.ppermute(value, axis, pairs)]
    reduce_sum x4 -> x0, other arithmetic: 4.93 us -> none  [the longest x2 3.65 us: shards(): power_new = jnp.sum(moved_probe * moved_probe)]
    add x6 -> x0, other arithmetic: 4.29 us -> none  [the longest x2 2.18 us: shards(): narrowed[:, :, :margin] + rim_right]
  transfers between devices with their start and end apart: 10 -> 0, of which waited for: 7 -> 0; matrix products, arithmetic and copies ran while one was open for 3% -> 0% of each run, Pallas kernels for 0% -> 0%
where the time goes in v1:
time: 81.1 us; the launch traced here: 80.9 us
  Pallas kernels  75.7 us (93%)
  local copies, waits for them, and re-layouts  3.68 us (5%)
  between operations  1.51 us (2%)
    pallas_call x2, Pallas kernels, exchanged(): pl.pallas_call(functools.partial(exchange_kernel, len(rim_scratch), last)...  57.3 us
    pallas_call x1, Pallas kernels, begin(): pl.pallas_call(halo_kernel, out_shape=jax.ShapeDtypeStruct((2, tile_rows...  9.23 us
    pallas_call x2, Pallas kernels, one_pass(): pl.pallas_call(pass_kernel, out_shape=(jax.ShapeDtypeStruct(extended.shap...  9.19 us
    unnamed x14, local copies, waits for them, and re-layouts  3.68 us

profile of v1, /device:TPU:25, one launch (start us, length us, event | category | flops | bytes accessed | tf_op | source)
XLA Modules:
  0.0 80.9 jit_solution(3698717540213444138)
XLA Ops:
  0.6 0.0 copy-start
  0.6 0.0 copy-start.1
  1.4 0.0 copy-start.4
  1.4 1.0 %copy-done.4 = f32[2,256,256]{2,1,0:T(8,128)S(1)} copy-done((f32[2,256,256]{2,1,0:T(8,128)S(1)}, f32[2,256,256]{2,1,0:T(8,128)}, u32[]{:S(2)}) %copy-start.4) | copy-done | bytes 524312
  2.5 0.0 copy-start.5
  2.5 9.2 %first_halo.1.ext_ref = f32[2,384,384]{2,1,0:T(8,128)S(1)} custom-call(f32[2,256,256]{2,1,0:T(8,128)S(1)} %copy-done.4), custom_call_target="tpu_custom_call" | custom-call | tf_op jit(solution)/shard_map/first_halo/pallas_call | solution.py:693
  11.7 0.0 copy-done
  11.7 0.0 copy-done.1
  11.7 0.0 copy-done.5
  11.7 0.0 copy-start.2
  11.7 1.0 %copy-done.2 = f32[2,256,256]{2,1,0:T(8,128)S(1)} copy-done((f32[2,256,256]{2,1,0:T(8,128)S(1)}, f32[2,256,256]{2,1,0:T(8,128)}, u32[]{:S(2)}) %copy-start.2) | copy-done | bytes 524312
  12.8 4.6 %window_pass.2 = (f32[2,384,384]{2,1,0:T(8,128)S(1)}, f32[2,256,256]{2,1,0:T(8,128)S(1)}, f32[8,256]{1,0:T(8,128)S(1)}) custom-call(s32[1,1,2,2]{3,2,1,0:T(2,128)S(1)} %copy-done.5, s32[1,1]{1,0:T(1,128)S(6)} %copy.10.cnt_ref, f32[2,384,384]{2,1,0:T(8,128)S(1)} %first_halo.1.ext_ref, f32[2,256,256]{2,1,0:T(8,128)S(1)} %copy-done.1, ...), custom_call_target="tpu_custom_call" | custom-call | tf_op jit(solution)/shard_map/window_pass/pallas_call | solution.py:225
  17.4 0.0 copy-start.3
  17.4 29.7 %exchange.1 = (f32[2,384,384]{2,1,0:T(8,128)S(1)}, f32[2,256,256]{2,1,0:T(8,128)S(1)}) custom-call(f32[2,384,384]{2,1,0:T(8,128)S(1)} %get-tuple-element.10.grad_ref, f32[2,256,256]{2,1,0:T(8,128)S(1)} %get-tuple-element.11.pgrad_ref, f32[8,256]{1,0:T(8,128)S(1)} %get-tuple-element.12.power_ref, f32[2,384,384]{2,1,0:T(8,128)S(1)} %first_halo.1.ext_ref, ...), custom_call_target="tpu_custom_call" | custom-call | tf_op jit(solution)/shard_map/exchange/pallas_call | solution.py:710
  47.1 0.0 copy-done.3
  47.1 4.6 %window_pass.3 = (f32[2,384,384]{2,1,0:T(8,128)S(1)}, f32[2,256,256]{2,1,0:T(8,128)S(1)}, f32[8,256]{1,0:T(8,128)S(1)}) custom-call(s32[1,1,2,2]{3,2,1,0:T(2,128)S(1)} %copy-done.5, s32[1,1]{1,0:T(1,128)S(6)} %copy.10.cnt_ref, f32[2,384,384]{2,1,0:T(8,128)S(1)} %get-tuple-element.13.ext_ref, f32[2,256,256]{2,1,0:T(8,128)S(1)} %get-tuple-element.14.probe_ref, ...), custom_call_target="tpu_custom_call" | custom-call | tf_op jit(solution)/shard_map/window_pass/pallas_call | solution.py:225
  51.7 27.6 %last_exchange.1 = (f32[2,256,256]{2,1,0:T(8,128)S(1)}, f32[2,256,256]{2,1,0:T(8,128)S(1)}) custom-call(f32[2,384,384]{2,1,0:T(8,128)S(1)} %get-tuple-element.15.grad_ref, f32[2,256,256]{2,1,0:T(8,128)S(1)} %get-tuple-element.16.pgrad_ref, f32[8,256]{1,0:T(8,128)S(1)} %get-tuple-element.17.power_ref, f32[2,384,384]{2,1,0:T(8,128)S(1)} %get-tuple-element.13.ext_ref, ...), custom_call_target="tpu_custom_call" | custom-call | tf_op jit(solution)/shard_map/last_exchange/pallas_call | solution.py:710
  79.3 0.8 copy.11
  80.1 0.8 copy.12
Async XLA Ops:
  0.6 11.1 %copy-start = (bf16[9,256,256]{2,1,0:T(8,128)(2,1)S(1)}, bf16[9,256,256]{2,1,0:T(8,128)(2,1)}, u32[]{:S(2)}) copy-start(bf16[9,256,256]{2,1,0:T(8,128)(2,1)} %constant.2.clone.tables) | copy-start | bytes 3538948
  0.6 11.1 %copy-start.1 = (f32[2,256,256]{2,1,0:T(8,128)S(1)}, f32[2,256,256]{2,1,0:T(8,128)}, u32[]{:S(2)}) copy-start(f32[2,256,256]{2,1,0:T(8,128)} %probe_ref.3) | copy-start | bytes 1572868
  1.4 1.0 %copy-start.4 = (f32[2,256,256]{2,1,0:T(8,128)S(1)}, f32[2,256,256]{2,1,0:T(8,128)}, u32[]{:S(2)}) copy-start(f32[2,256,256]{2,1,0:T(8,128)} %object_ref.1) | copy-start | bytes 1572868
  2.5 9.3 %copy-start.5 = (s32[1,1,2,2]{3,2,1,0:T(2,128)S(1)}, s32[1,1,2,2]{3,2,1,0:T(2,128)}, u32[]{:S(2)}) copy-start(s32[1,1,2,2]{3,2,1,0:T(2,128)} %off_ref.3) | copy-start | bytes 52
  11.7 1.0 %copy-start.2 = (f32[2,256,256]{2,1,0:T(8,128)S(1)}, f32[2,256,256]{2,1,0:T(8,128)}, u32[]{:S(2)}) copy-start(f32[2,256,256]{2,1,0:T(8,128)} %amp_ref.3) | copy-start | bytes 1572868
  17.4 29.7 %copy-start.3 = (f32[2,256,256]{2,1,0:T(8,128)S(1)}, f32[2,256,256]{2,1,0:T(8,128)}, u32[]{:S(2)}) copy-start(f32[2,256,256]{2,1,0:T(8,128)} %amp_ref.3) | copy-start | bytes 1572868

commit v2 on v1

--- a/solution.py
+++ b/solution.py
@@ -118,19 +118,17 @@
     return lanes(left_re, right_re), lanes(left_im, right_im)
 
 
-def sorted_amplitudes(amp_ref, slot, tables, hold):
-    upper, lower = split(amp_ref[slot])
-    value = dot(upper, tables[8]) + dot(lower, tables[8])
-    left, right = halves_of_lanes(value)
-    hold[0] = left
-    hold[1] = right
-    half = value.shape[0] // 2
-    return [
-        lanes(
-            hold[0, pl.ds(parity, half, stride=2), :], hold[1, pl.ds(parity, half, stride=2), :]
-        )
-        for parity in range(2)
-    ]
+def sort_amplitudes(amp_ref, tables, hold, ordered):
+    half = hold.shape[2] // 2
+    for slot in range(amp_ref.shape[0]):
+        upper, lower = split(amp_ref[slot])
+        value = dot(upper, tables[8]) + dot(lower, tables[8])
+        for side, part in enumerate(halves_of_lanes(value)):
+            hold[slot, side] = part
+            for parity in range(2):
+                ordered[slot, parity, :, side * half : (side + 1) * half] = hold[
+                    slot, side, pl.ds(parity, half, stride=2), :
+                ]
 
 
 def cut_window(slabs, part, first_row, first_col, window, margin):
@@ -157,9 +155,9 @@
 
 
 def pass_over_windows(
-    off_ref, cnt_ref, ext_ref, probe_ref, amp_ref, tables, grad_ref, pgrad_ref, hold, slabs, padded
+    off_ref, cnt_ref, ext_ref, probe_ref, ordered, tables, grad_ref, pgrad_ref, slabs, padded
 ):
-    slot_count = amp_ref.shape[0]
+    slot_count = ordered.shape[0]
     window = probe_ref.shape[1]
     ext_rows = ext_ref.shape[1]
     margin = ext_rows - window
@@ -179,7 +177,8 @@
             probe_re * win_re - probe_im * win_im, probe_re * win_im + probe_im * win_re, tables
         )
         replaced = []
-        for hat, measured in zip(spectrum, sorted_amplitudes(amp_ref, slot, tables, hold.at[slot])):
+        for parity, hat in enumerate(spectrum):
+            measured = ordered[slot, parity]
             hat_re, hat_im = halves_of_rows(hat)
             ratio = measured * lax.rsqrt(hat_re * hat_re + hat_im * hat_im + smooth_floor) - 1.0
             ratio = ratio * live
@@ -210,16 +209,27 @@
 def pass_kernel(
     off_ref, cnt_ref, ext_ref, probe_ref, amp_ref, tables, grad_ref, pgrad_ref, power_ref, *scratch
 ):
+    hold, ordered, slabs, padded = scratch
+    sort_amplitudes(amp_ref, tables, hold, ordered)
     power = pass_over_windows(
-        off_ref, cnt_ref, ext_ref, probe_ref, amp_ref, tables, grad_ref, pgrad_ref, *scratch
+        off_ref, cnt_ref, ext_ref, probe_ref, ordered, tables, grad_ref, pgrad_ref, slabs, padded
     )
     power_ref[...] = jnp.broadcast_to(power, power_ref.shape)
+
+
+def pass_scratch(slots, window, ext_rows, ext_cols):
+    margin = ext_rows - window
+    return [
+        pltpu.VMEM((slots, 2, window, window // 2), jnp.float32),
+        pltpu.VMEM((slots, 2, window // 2, window), jnp.float32),
+        pltpu.VMEM((2, ext_cols // margin, ext_rows, margin), jnp.float32),
+        pltpu.VMEM((slots, 2, ext_cols // margin, window + 2 * margin, margin), jnp.float32),
+    ]
 
 
 def one_pass(extended, probe, amplitudes, offsets, counts, tables):
     slots, window = amplitudes.shape[0], probe.shape[1]
     ext_rows, ext_cols = extended.shape[1:]
-    margin = ext_rows - window
     smem = pl.BlockSpec(memory_space=pltpu.SMEM)
     vmem = pl.BlockSpec(memory_space=pltpu.VMEM)
     return pl.pallas_call(
@@ -231,11 +241,7 @@
         ),
         in_specs=[smem, smem, vmem, vmem, vmem, vmem],
         out_specs=(vmem, vmem, vmem),
-        scratch_shapes=[
-            pltpu.VMEM((slots, 2, window, window // 2), jnp.float32),
-            pltpu.VMEM((2, ext_cols // margin, ext_rows, margin), jnp.float32),
-            pltpu.VMEM((slots, 2, ext_cols // margin, window + 2 * margin, margin), jnp.float32),
-        ],
+        scratch_shapes=pass_scratch(slots, window, ext_rows, ext_cols),
         compiler_params=pltpu.CompilerParams(vmem_limit_bytes=40 * 2**20),
         name="window_pass",
     )(offsets, counts, extended, probe, amplitudes, tables)
@@ -499,7 +505,7 @@
 
 
 class Sums:
-    extra = 8
+    extra = 1
 
     @staticmethod
     def chunk(rows, cols, window):
@@ -644,26 +650,46 @@
                 copy.wait_send()
 
 
-def halo_kernel(object_ref, ext_ref, *scratch):
+def whole_kernel(
+    counts_of, off_ref, cnt_ref, object_ref, probe_ref, amp_hbm, tab_hbm, out_ref, new_ref, *scratch
+):
+    scratch = list(scratch)
+    groups = []
+    for count in counts_of:
+        groups.append(scratch[:count])
+        del scratch[:count]
+    own, pass_refs, halo_refs, *step_refs = groups
+    amp_ref, tab_ref, loads, ext_a, ext_b, probe_b, grad_ref, pgrad_ref = own
+    hold, ordered, slabs, padded = pass_refs
     place = Place()
     place.greet()
-    halo = Halo(place, object_ref, *scratch)
+    amp_load = pltpu.make_async_copy(amp_hbm, amp_ref, loads.at[0])
+    tab_load = pltpu.make_async_copy(tab_hbm, tab_ref, loads.at[1])
+    amp_load.start()
+    tab_load.start()
+    halo = Halo(place, object_ref, *halo_refs)
     place.await_greetings()
     halo.start()
-    halo.finish(ext_ref)
+    amp_load.wait()
+    tab_load.wait()
+    sort_amplitudes(amp_ref, tab_ref, hold, ordered)
+    halo.finish(ext_a)
+    exts, probes = [ext_a, ext_b], [probe_ref, probe_b]
+    for step in range(OUTER):
+        last = step == OUTER - 1
+        ext, probe = exts[step % 2], probes[step % 2]
+        power = pass_over_windows(
+            off_ref, cnt_ref, ext, probe, ordered, tab_ref, grad_ref, pgrad_ref, slabs, padded
+        )
+        rim_refs, sum_refs = step_refs[2 * step : 2 * step + 2]
+        rims = Rims(place, last, grad_ref, *rim_refs)
+        sums = Sums(place, *sum_refs)
+        sums.fill(pgrad_ref, power)
+        if last:
+            exchange(rims, sums, ext, probe, out_ref, new_ref)
+        else:
+            exchange(rims, sums, ext, probe, exts[1 - step % 2], probes[1 - step % 2])
     halo.settle()
-
-
-def exchange_kernel(
-    rim_scratch, last, grad_ref, pgrad_ref, power_ref, ext_ref, probe_ref, out_ref, new_ref, *scratch
-):
-    place = Place()
-    place.greet()
-    rims = Rims(place, last, grad_ref, *scratch[:rim_scratch])
-    sums = Sums(place, *scratch[rim_scratch:])
-    sums.fill(pgrad_ref, power_ref[0:1])
-    place.await_greetings()
-    exchange(rims, sums, ext_ref, probe_ref, out_ref, new_ref)
 
 
 def exchange(rims, sums, ext_ref, probe_ref, out_ref, new_ref):
@@ -681,54 +707,43 @@
     sums.settle()
 
 
-def kernel_params(number):
-    return pltpu.CompilerParams(
-        collective_id=number, has_side_effects=True, vmem_limit_bytes=40 * 2**20
-    )
-
-
-def begin(object_field, margin):
+def shards_by_kernel(object_field, probe_field, amplitudes, offsets, counts):
+    tables = jnp.asarray(make_tables(probe_field.shape[1]))
     _, tile_rows, tile_cols = object_field.shape
+    slots, window = amplitudes.shape[0], probe_field.shape[1]
+    rows, cols = lax.axis_size("row"), lax.axis_size("col")
+    extended = (2, tile_rows + HALO, tile_cols + HALO)
+    own = [
+        pltpu.VMEM(amplitudes.shape, jnp.float32),
+        pltpu.VMEM(tables.shape, jnp.bfloat16),
+        pltpu.SemaphoreType.DMA((2,)),
+        pltpu.VMEM(extended, jnp.float32),
+        pltpu.VMEM(extended, jnp.float32),
+        pltpu.VMEM(probe_field.shape, jnp.float32),
+        pltpu.VMEM(extended, jnp.float32),
+        pltpu.VMEM(probe_field.shape, jnp.float32),
+    ]
+    groups = [own, pass_scratch(slots, window, *extended[1:]), Halo.scratch(tile_rows, tile_cols, HALO)]
+    for step in range(OUTER):
+        groups.append(Rims.scratch(tile_rows, tile_cols, HALO))
+        groups.append(Sums.scratch(rows, cols, window))
+    smem = pl.BlockSpec(memory_space=pltpu.SMEM)
     vmem = pl.BlockSpec(memory_space=pltpu.VMEM)
+    anywhere = pl.BlockSpec(memory_space=pl.ANY)
     return pl.pallas_call(
-        halo_kernel,
-        out_shape=jax.ShapeDtypeStruct((2, tile_rows + margin, tile_cols + margin), jnp.float32),
-        in_specs=[vmem],
-        out_specs=vmem,
-        scratch_shapes=Halo.scratch(tile_rows, tile_cols, margin),
-        compiler_params=kernel_params(0),
-        name="first_halo",
-    )(object_field)
-
-
-def exchanged(last, margin, grad_ext, probe_grad, power, extended, probe):
-    tile_rows, tile_cols = extended.shape[1] - margin, extended.shape[2] - margin
-    rows, cols, window = lax.axis_size("row"), lax.axis_size("col"), probe.shape[1]
-    vmem = pl.BlockSpec(memory_space=pltpu.VMEM)
-    rim_scratch = Rims.scratch(tile_rows, tile_cols, margin)
-    out = (2, tile_rows, tile_cols) if last else extended.shape
-    return pl.pallas_call(
-        functools.partial(exchange_kernel, len(rim_scratch), last),
+        functools.partial(whole_kernel, [len(group) for group in groups]),
         out_shape=(
-            jax.ShapeDtypeStruct(out, jnp.float32),
-            jax.ShapeDtypeStruct(probe.shape, jnp.float32),
+            jax.ShapeDtypeStruct(object_field.shape, jnp.float32),
+            jax.ShapeDtypeStruct(probe_field.shape, jnp.float32),
         ),
-        in_specs=[vmem] * 5,
+        in_specs=[smem, smem, vmem, vmem, anywhere, anywhere],
         out_specs=(vmem, vmem),
-        scratch_shapes=rim_scratch + Sums.scratch(rows, cols, window),
-        compiler_params=kernel_params(2 if last else 1),
-        name="last_exchange" if last else "exchange",
-    )(grad_ext, probe_grad, power, extended, probe)
-
-
-def shards_by_kernels(object_field, probe_field, amplitudes, offsets, counts):
-    tables = jnp.asarray(make_tables(probe_field.shape[1]))
-    extended = begin(object_field, HALO)
-    probe = probe_field
-    for outer_step in range(OUTER):
-        terms = one_pass(extended, probe, amplitudes, offsets, counts, tables)
-        extended, probe = exchanged(outer_step == OUTER - 1, HALO, *terms, extended, probe)
-    return (extended, probe)
+        scratch_shapes=sum(groups, []),
+        compiler_params=pltpu.CompilerParams(
+            collective_id=0, has_side_effects=True, vmem_limit_bytes=50 * 2**20
+        ),
+        name="refinement",
+    )(offsets, counts, object_field, probe_field, amplitudes, tables)
 
 
 def shards(object_field, probe_field, amplitudes, offsets, counts):
@@ -773,7 +788,7 @@
 
     def shards_here(*args):
         deep = Sums.chunk(rows, cols, args[1].shape[1])
-        return (shards_by_kernels if deep and deep % 8 == 0 else shards)(*args)
+        return (shards_by_kernel if deep and deep % 8 == 0 else shards)(*args)
 
     return jax.shard_map(
         shards_here,

time: 81.1 us -> 75.4 us (0.930)
  Pallas kernels: 75.7 us -> 67.2 us
  local copies, waits for them, and re-layouts: 3.68 us -> 6.66 us
    pallas_call x5 -> x1, Pallas kernels: 75.7 us -> 67.2 us  [shards_by_kernel(): pl.pallas_call(functools.partial(whole_kernel, [len(group) for group in g...]
    unnamed x14 -> x12, local copies, waits for them, and re-layouts: 3.68 us -> 6.66 us
where the time goes in v2:
time: 75.4 us; the launch traced here: 75.1 us
  Pallas kernels  67.2 us (89%)
  local copies, waits for them, and re-layouts  6.66 us (9%)
  between operations  1.3 us (2%)
    pallas_call x1, Pallas kernels, shards_by_kernel(): pl.pallas_call(functools.partial(whole_kernel, [len(group) for group in g...  67.2 us
    unnamed x12, local copies, waits for them, and re-layouts  6.66 us

profile of v2, /device:TPU:25, one launch (start us, length us, event | category | flops | bytes accessed | tf_op | source)
XLA Modules:
  0.0 75.1 jit_solution(3148334441611180872)
XLA Ops:
  1.3 0.0 copy-start
  1.3 1.3 %copy-done = bf16[9,256,256]{2,1,0:T(8,128)(2,1)S(1)} copy-done((bf16[9,256,256]{2,1,0:T(8,128)(2,1)S(1)}, bf16[9,256,256]{2,1,0:T(8,128)(2,1)}, u32[]{:S(2)}) %copy-start) | copy-done | bytes 1179672
  2.6 0.0 copy-start.1
  2.6 1.0 %copy-done.1 = f32[2,256,256]{2,1,0:T(8,128)S(1)} copy-done((f32[2,256,256]{2,1,0:T(8,128)S(1)}, f32[2,256,256]{2,1,0:T(8,128)}, u32[]{:S(2)}) %copy-start.1) | copy-done | bytes 524312
  3.6 0.0 copy-start.2
  3.6 1.0 %copy-done.2 = f32[2,256,256]{2,1,0:T(8,128)S(1)} copy-done((f32[2,256,256]{2,1,0:T(8,128)S(1)}, f32[2,256,256]{2,1,0:T(8,128)}, u32[]{:S(2)}) %copy-start.2) | copy-done | bytes 524312
  4.6 0.0 copy-start.3
  4.6 1.0 %copy-done.3 = f32[2,256,256]{2,1,0:T(8,128)S(1)} copy-done((f32[2,256,256]{2,1,0:T(8,128)S(1)}, f32[2,256,256]{2,1,0:T(8,128)}, u32[]{:S(2)}) %copy-start.3) | copy-done | bytes 524312
  5.7 0.0 copy-start.4
  5.7 0.7 copy-done.4
  6.4 67.2 %refinement.1 = (f32[2,256,256]{2,1,0:T(8,128)S(1)}, f32[2,256,256]{2,1,0:T(8,128)S(1)}) custom-call(s32[1,1,2,2]{3,2,1,0:T(2,128)S(1)} %copy-done.4, s32[1,1]{1,0:T(1,128)S(6)} %copy.10.cnt_ref, f32[2,256,256]{2,1,0:T(8,128)S(1)} %copy-done.1, f32[2,256,256]{2,1,0:T(8,128)S(1)} %copy-done.2, f32[2,256,256]{2,1,0:T(8,128)S(1)} %copy-done.3, ...), custom_call_target="tpu_custom_call" | custom-call | tf_op jit(solution)/shard_map/refinement/pallas_call | solution.py:733
  73.5 0.8 %copy.11 = f32[2,256,256]{2,1,0:T(8,128)} copy(f32[2,256,256]{2,1,0:T(8,128)S(1)} %get-tuple-element.4) | data formatting | bytes 1048576
  74.3 0.8 %copy.12 = f32[2,256,256]{2,1,0:T(8,128)} copy(f32[2,256,256]{2,1,0:T(8,128)S(1)} %get-tuple-element.5) | data formatting | bytes 1048576
Async XLA Ops:
  1.3 1.3 %copy-start = (bf16[9,256,256]{2,1,0:T(8,128)(2,1)S(1)}, bf16[9,256,256]{2,1,0:T(8,128)(2,1)}, u32[]{:S(2)}) copy-start(bf16[9,256,256]{2,1,0:T(8,128)(2,1)} %constant.2.clone.tab_hbm) | copy-start | bytes 3538948
  2.6 1.0 %copy-start.1 = (f32[2,256,256]{2,1,0:T(8,128)S(1)}, f32[2,256,256]{2,1,0:T(8,128)}, u32[]{:S(2)}) copy-start(f32[2,256,256]{2,1,0:T(8,128)} %object_ref.1) | copy-start | bytes 1572868
  3.6 1.0 %copy-start.2 = (f32[2,256,256]{2,1,0:T(8,128)S(1)}, f32[2,256,256]{2,1,0:T(8,128)}, u32[]{:S(2)}) copy-start(f32[2,256,256]{2,1,0:T(8,128)} %probe_ref.1) | copy-start | bytes 1572868
  4.6 1.0 %copy-start.3 = (f32[2,256,256]{2,1,0:T(8,128)S(1)}, f32[2,256,256]{2,1,0:T(8,128)}, u32[]{:S(2)}) copy-start(f32[2,256,256]{2,1,0:T(8,128)} %amp_hbm.1) | copy-start | bytes 1572868
  5.7 0.7 copy-start.4

commit v3 on v2

--- a/solution.py
+++ b/solution.py
@@ -511,27 +511,46 @@
     def chunk(rows, cols, window):
         return 2 * window * window // 128 // (rows * cols)
 
+    @staticmethod
+    def group(rows):
+        return max(size for size in range(1, rows + 1) if rows % size == 0 and size * size <= rows)
+
     @classmethod
     def scratch(cls, rows, cols, window):
         deep = cls.chunk(rows, cols, window)
         full = deep + cls.extra
-        more_cols, more_rows = max(cols - 1, 1), rows - 1
+        near = cls.group(rows)
+        far = rows // near
+        more_cols, more_near, more_far = (max(size - 1, 1) for size in (cols, near, far))
         return [
-            pltpu.VMEM((cols, rows, full, 128), jnp.float32),
-            pltpu.VMEM((more_cols, rows, full, 128), jnp.float32),
-            pltpu.VMEM((rows, full, 128), jnp.float32),
-            pltpu.VMEM((more_rows, full, 128), jnp.float32),
-            pltpu.VMEM((cols, rows, deep, 128), jnp.float32),
+            pltpu.VMEM((cols, near, far, full, 128), jnp.float32),
+            pltpu.VMEM((more_cols, near, far, full, 128), jnp.float32),
+            pltpu.VMEM((near, far, full, 128), jnp.float32),
+            pltpu.VMEM((more_near, far, full, 128), jnp.float32),
+            pltpu.VMEM((far, full, 128), jnp.float32),
+            pltpu.VMEM((more_far, full, 128), jnp.float32),
+            pltpu.VMEM((cols, near, far, deep, 128), jnp.float32),
             pltpu.SemaphoreType.DMA((2, more_cols)),
-            pltpu.SemaphoreType.DMA((2, more_rows)),
-            pltpu.SemaphoreType.DMA((2, more_rows)),
-            pltpu.SemaphoreType.DMA((2, more_cols, rows)),
+            pltpu.SemaphoreType.DMA((2, 2, more_near)),
+            pltpu.SemaphoreType.DMA((2, 2, more_far)),
+            pltpu.SemaphoreType.DMA((2, more_cols, near)),
         ]
 
-    def __init__(self, place, whole, from_cols, part, from_rows, gathered, sems, sems2, sems3, sems4):
+    def __init__(
+        self, place, whole, from_cols, part, from_near, less, from_far, gathered, sems, sems2, sems3, sems4
+    ):
         self.place, self.whole, self.from_cols, self.part = place, whole, from_cols, part
-        self.from_rows, self.gathered = from_rows, gathered
-        self.deep = gathered.shape[2]
+        self.from_near, self.less, self.from_far, self.gathered = from_near, less, from_far, gathered
+        _, self.near, self.far, self.deep, _ = gathered.shape
+        near, far = self.near, self.far
+        self.at_far, self.at_near = place.row // near, lax.rem(place.row, near)
+
+        def other_near(step):
+            return lax.rem(self.at_near + step, near)
+
+        def other_far(step):
+            return lax.rem(self.at_far + step, far)
+
         self.over_cols = [
             remote(
                 whole.at[place.other_col(step)],
@@ -542,35 +561,56 @@
             )
             for step in range(1, place.cols)
         ]
-        self.over_rows = [
+        self.over_near = [
             remote(
-                part.at[place.other_row(step)],
-                from_rows.at[step - 1],
-                sems2.at[0, step - 1],
-                sems2.at[1, step - 1],
-                row=place.other_row(step),
-            )
-            for step in range(1, place.rows)
+                part.at[other_near(step)],
+                from_near.at[step - 1],
+                sems2.at[0, 0, step - 1],
+                sems2.at[0, 1, step - 1],
+                row=self.at_far * near + other_near(step),
+            )
+            for step in range(1, near)
         ]
-        mine = gathered.at[place.col, place.row]
-        self.back_rows = [
+        self.over_far = [
+            remote(
+                less.at[other_far(step)],
+                from_far.at[step - 1],
+                sems3.at[0, 0, step - 1],
+                sems3.at[0, 1, step - 1],
+                row=other_far(step) * near + self.at_near,
+            )
+            for step in range(1, far)
+        ]
+        mine = gathered.at[place.col, self.at_near, self.at_far]
+        self.back_far = [
             remote(
                 mine,
                 mine,
-                sems3.at[0, step - 1],
-                sems3.at[1, step - 1],
-                row=place.other_row(step),
-            )
-            for step in range(1, place.rows)
+                sems3.at[1, 0, step - 1],
+                sems3.at[1, 1, step - 1],
+                row=other_far(step) * near + self.at_near,
+            )
+            for step in range(1, far)
+        ]
+        block = gathered.at[place.col, self.at_near]
+        self.back_near = [
+            remote(
+                block,
+                block,
+                sems2.at[1, 0, step - 1],
+                sems2.at[1, 1, step - 1],
+                row=self.at_far * near + other_near(step),
+            )
+            for step in range(1, near)
         ]
         self.back_cols = []
-        for step in range(place.rows):
-            chunk = gathered.at[place.col, place.other_row(place.rows - step)]
+        for step in range(near):
+            block = gathered.at[place.col, other_near(near - step)]
             self.back_cols.append(
                 [
                     remote(
-                        chunk,
-                        chunk,
+                        block,
+                        block,
                         sems4.at[0, other - 1, step],
                         sems4.at[1, other - 1, step],
                         col=place.other_col(other),
@@ -583,46 +623,61 @@
         per = window // self.deep
         for number in range(self.place.cols * self.place.rows):
             slab, at = divmod(number, per)
-            half, col = divmod(slab, window // 128)
-            yield half, col * 128, at * self.deep, number // self.place.rows, number % self.place.rows
+            half, side = divmod(slab, window // 128)
+            here = (
+                half,
+                slice(at * self.deep, (at + 1) * self.deep),
+                slice(side * 128, (side + 1) * 128),
+            )
+            rest, far = divmod(number, self.far)
+            yield here, (rest // self.near, rest % self.near, far)
 
     def fill(self, pgrad_ref, power):
         window = pgrad_ref.shape[1]
-        for half, lane, line, col, row in self.slots(window):
-            self.whole[col, row, : self.deep] = pgrad_ref[
-                half, line : line + self.deep, lane : lane + 128
-            ]
         folded = sum(power[:, at : at + 128] for at in range(0, window, 128))
-        first = lax.broadcasted_iota(jnp.int32, (self.extra, 128), 0) == 0
-        block = jnp.where(first, jnp.broadcast_to(folded, (self.extra, 128)), 0.0)
-        for col in range(self.place.cols):
-            for row in range(self.place.rows):
-                self.whole[col, row, self.deep :] = block
+        for here, (col, near, far) in self.slots(window):
+            self.whole[col, near, far, : self.deep] = pgrad_ref[here]
+            self.whole[col, near, far, self.deep :] = folded
 
     def start(self):
         for copy in self.over_cols:
             copy.start()
 
-    def start_rows(self):
+    def start_near(self):
         self.part[...] = self.whole[self.place.col]
         for step, copy in enumerate(self.over_cols):
             copy.wait_recv()
             self.part[...] += self.from_cols[step]
-        for copy in self.over_rows:
+        for copy in self.over_near:
             copy.start()
 
+    def start_far(self):
+        total = self.part[self.at_near]
+        for step, copy in enumerate(self.over_near):
+            copy.wait_recv()
+            total = total + self.from_near[step]
+        self.less[...] = total
+        for copy in self.over_far:
+            copy.start()
+
     def start_back(self):
-        total = self.part[self.place.row]
-        for step, copy in enumerate(self.over_rows):
+        total = self.less[self.at_far]
+        for step, copy in enumerate(self.over_far):
             copy.wait_recv()
-            total = total + self.from_rows[step]
-        self.gathered[self.place.col, self.place.row] = total[: self.deep]
-        for copy in self.back_rows + self.back_cols[0]:
+            total = total + self.from_far[step]
+        self.gathered[self.place.col, self.at_near, self.at_far] = total[: self.deep]
+        for copy in self.back_far:
             copy.start()
         return jnp.sum(total[self.deep :])
 
+    def start_back_near(self):
+        for copy in self.back_far:
+            copy.wait_recv()
+        for copy in self.back_near + self.back_cols[0]:
+            copy.start()
+
     def pass_on(self):
-        for step, copy in enumerate(self.back_rows):
+        for step, copy in enumerate(self.back_near):
             copy.wait_recv()
             for other in self.back_cols[step + 1]:
                 other.start()
@@ -634,24 +689,20 @@
                 copy.wait_recv()
         old = jnp.sum(probe_ref[...] * probe_ref[...], keepdims=True)
         scale = 1.0 / (power / (window * window) + tiny_value)
-        for half, lane, line, col, row in self.slots(window):
-            here = (half, slice(line, line + self.deep), slice(lane, lane + 128))
-            moved = probe_ref[here] + self.gathered[col, row] * scale
-            new_ref[here] = moved
+        for here, (col, near, far) in self.slots(window):
+            new_ref[here] = probe_ref[here] + self.gathered[col, near, far] * scale
         moved = new_ref[...]
         new = jnp.sum(moved * moved, keepdims=True)
         new_ref[...] = moved * jnp.sqrt(old / (new + tiny_value))
 
     def settle(self):
-        for copy in self.over_cols + self.over_rows + self.back_rows:
+        copies = self.over_cols + self.over_near + self.over_far + self.back_far + self.back_near
+        for copy in copies + sum(self.back_cols, []):
             copy.wait_send()
-        for copies in self.back_cols:
-            for copy in copies:
-                copy.wait_send()
 
 
 def whole_kernel(
-    counts_of, off_ref, cnt_ref, object_ref, probe_ref, amp_hbm, tab_hbm, out_ref, new_ref, *scratch
+    counts_of, off_ref, cnt_ref, object_hbm, probe_hbm, amp_hbm, tab_hbm, out_ref, new_ref, *scratch
 ):
     scratch = list(scratch)
     groups = []
@@ -659,19 +710,25 @@
         groups.append(scratch[:count])
         del scratch[:count]
     own, pass_refs, halo_refs, *step_refs = groups
-    amp_ref, tab_ref, loads, ext_a, ext_b, probe_b, grad_ref, pgrad_ref = own
+    object_ref, probe_ref, amp_ref, tab_ref, loads, ext_a, ext_b, probe_b, grad_ref, pgrad_ref = own
     hold, ordered, slabs, padded = pass_refs
     place = Place()
     place.greet()
-    amp_load = pltpu.make_async_copy(amp_hbm, amp_ref, loads.at[0])
-    tab_load = pltpu.make_async_copy(tab_hbm, tab_ref, loads.at[1])
-    amp_load.start()
-    tab_load.start()
+    pairs = (
+        (object_hbm, object_ref),
+        (tab_hbm, tab_ref),
+        (amp_hbm, amp_ref),
+        (probe_hbm, probe_ref),
+    )
+    copies = [pltpu.make_async_copy(*pair, loads.at[at]) for at, pair in enumerate(pairs)]
+    for copy in copies:
+        copy.start()
     halo = Halo(place, object_ref, *halo_refs)
     place.await_greetings()
+    copies[0].wait()
     halo.start()
-    amp_load.wait()
-    tab_load.wait()
+    for copy in copies[1:]:
+        copy.wait()
     sort_amplitudes(amp_ref, tab_ref, hold, ordered)
     halo.finish(ext_a)
     exts, probes = [ext_a, ext_b], [probe_ref, probe_b]
@@ -696,9 +753,11 @@
     window = probe_ref.shape[1]
     sums.start()
     rims.start()
-    sums.start_rows()
+    sums.start_near()
+    sums.start_far()
     rims.start_rows()
     power = sums.start_back()
+    sums.start_back_near()
     mean = jnp.sum(probe_ref[...] * probe_ref[...]) / (window * window)
     rims.finish(ext_ref, out_ref, object_step / (mean + tiny_value))
     sums.pass_on()
@@ -714,9 +773,11 @@
     rows, cols = lax.axis_size("row"), lax.axis_size("col")
     extended = (2, tile_rows + HALO, tile_cols + HALO)
     own = [
+        pltpu.VMEM(object_field.shape, jnp.float32),
+        pltpu.VMEM(probe_field.shape, jnp.float32),
         pltpu.VMEM(amplitudes.shape, jnp.float32),
         pltpu.VMEM(tables.shape, jnp.bfloat16),
-        pltpu.SemaphoreType.DMA((2,)),
+        pltpu.SemaphoreType.DMA((4,)),
         pltpu.VMEM(extended, jnp.float32),
         pltpu.VMEM(extended, jnp.float32),
         pltpu.VMEM(probe_field.shape, jnp.float32),
@@ -736,11 +797,11 @@
             jax.ShapeDtypeStruct(object_field.shape, jnp.float32),
             jax.ShapeDtypeStruct(probe_field.shape, jnp.float32),
         ),
-        in_specs=[smem, smem, vmem, vmem, anywhere, anywhere],
+        in_specs=[smem, smem, anywhere, anywhere, anywhere, anywhere],
         out_specs=(vmem, vmem),
         scratch_shapes=sum(groups, []),
         compiler_params=pltpu.CompilerParams(
-            collective_id=0, has_side_effects=True, vmem_limit_bytes=50 * 2**20
+            collective_id=0, has_side_effects=True, vmem_limit_bytes=60 * 2**20
         ),
         name="refinement",
     )(offsets, counts, object_field, probe_field, amplitudes, tables)

time: 75.4 us -> 71.8 us (0.952)
  local copies, waits for them, and re-layouts: 6.66 us -> 2.72 us
    unnamed x12 -> x4, local copies, waits for them, and re-layouts: 6.66 us -> 2.72 us
where the time goes in v3:
time: 71.8 us; the launch traced here: 71.2 us
  Pallas kernels  67.2 us (94%)
  local copies, waits for them, and re-layouts  2.72 us (4%)
  between operations  1.29 us (2%)
    pallas_call x1, Pallas kernels, shards_by_kernel(): pl.pallas_call(functools.partial(whole_kernel, [len(group) for group in g...  67.2 us
    unnamed x4, local copies, waits for them, and re-layouts  2.72 us

profile of v3, /device:TPU:25, one launch (start us, length us, event | category | flops | bytes accessed | tf_op | source)
XLA Modules:
  0.0 71.2 jit_solution(1205650255404074782)
XLA Ops:
  1.3 67.2 %refinement.1 = (f32[2,256,256]{2,1,0:T(8,128)}, f32[2,256,256]{2,1,0:T(8,128)}) custom-call(s32[1,1,2,2]{3,2,1,0:T(2,128)} %off_ref.1, s32[1,1]{1,0:T(1,128)S(6)} %copy.10.cnt_ref, f32[2,256,256]{2,1,0:T(8,128)} %object_hbm.1, f32[2,256,256]{2,1,0:T(8,128)} %probe_hbm.1, f32[2,256,256]{2,1,0:T(8,128)} %amp_hbm.1, bf16[9,256,256]{2,1,0:T(8,128)(2,1)} %constant.2.clone.tab_hbm), custom_call_target="tpu_custom_call" | custom-call | tf_op jit(solution)/shard_map/refinement/pallas_call | solution.py:794
  68.5 0.0 copy-start
  68.5 1.9 %copy.11 = f32[2,256,256]{2,1,0:T(8,128)} copy(f32[2,256,256]{2,1,0:T(8,128)} %get-tuple-element.4) | data formatting | bytes 1048576
  70.4 0.0 copy-done
  70.4 0.8 %copy.12 = f32[2,256,256]{2,1,0:T(8,128)} copy(f32[2,256,256]{2,1,0:T(8,128)S(1)} %copy-done) | data formatting | bytes 1048576
Async XLA Ops:
  68.5 1.9 %copy-start = (f32[2,256,256]{2,1,0:T(8,128)S(1)}, f32[2,256,256]{2,1,0:T(8,128)}, u32[]{:S(2)}) copy-start(f32[2,256,256]{2,1,0:T(8,128)} %get-tuple-element.5) | copy-start | bytes 1572868

commit v4 on v3

--- a/solution.py
+++ b/solution.py
@@ -155,7 +155,7 @@
 
 
 def pass_over_windows(
-    off_ref, cnt_ref, ext_ref, probe_ref, ordered, tables, grad_ref, pgrad_ref, slabs, padded
+    off_ref, cnt_ref, ext_ref, probe_ref, ordered, tables, grad_ref, pgrad_ref, slabs, padded, summed
 ):
     slot_count = ordered.shape[0]
     window = probe_ref.shape[1]
@@ -184,6 +184,13 @@
             ratio = ratio * live
             replaced.append(stack(hat_re * ratio, hat_im * ratio))
         diff_re, diff_im = inverse(*replaced, tables)
+        probe_terms = (win_re * diff_re + win_im * diff_im, win_re * diff_im - win_im * diff_re)
+        for part, term in enumerate(probe_terms):
+            pgrad_ref[part] = term if slot == 0 else pgrad_ref[part] + term
+        squares = jnp.sum(win_re * win_re + win_im * win_im, axis=0, keepdims=True) * live
+        power = squares if power is None else power + squares
+        if slot == slot_count - 1:
+            summed(power)
         terms = (probe_re * diff_re + probe_im * diff_im, probe_re * diff_im - probe_im * diff_re)
         for part, term in enumerate(terms):
             empty = jnp.zeros((margin, margin), jnp.float32)
@@ -198,12 +205,6 @@
                     grad_ref[part, :, here] = shown
                 else:
                     grad_ref[part, :, here] += shown
-        probe_terms = (win_re * diff_re + win_im * diff_im, win_re * diff_im - win_im * diff_re)
-        for part, term in enumerate(probe_terms):
-            pgrad_ref[part] = term if slot == 0 else pgrad_ref[part] + term
-        squares = jnp.sum(win_re * win_re + win_im * win_im, axis=0, keepdims=True) * live
-        power = squares if power is None else power + squares
-    return power
 
 
 def pass_kernel(
@@ -211,10 +212,13 @@
 ):
     hold, ordered, slabs, padded = scratch
     sort_amplitudes(amp_ref, tables, hold, ordered)
-    power = pass_over_windows(
-        off_ref, cnt_ref, ext_ref, probe_ref, ordered, tables, grad_ref, pgrad_ref, slabs, padded
+
+    def summed(power):
+        power_ref[...] = jnp.broadcast_to(power, power_ref.shape)
+
+    pass_over_windows(
+        off_ref, cnt_ref, ext_ref, probe_ref, ordered, tables, grad_ref, pgrad_ref, slabs, padded, summed
     )
-    power_ref[...] = jnp.broadcast_to(power, power_ref.shape)
 
 
 def pass_scratch(slots, window, ext_rows, ext_cols):
@@ -301,8 +305,8 @@
             pltpu.VMEM((2, margin, tile_cols), jnp.float32),
             pltpu.VMEM((2, tile_rows, margin), jnp.float32),
             pltpu.VMEM((2, margin, margin), jnp.float32),
-            pltpu.SemaphoreType.DMA((3,)),
-            pltpu.SemaphoreType.DMA((3,)),
+            pltpu.SemaphoreType.DMA((4,)),
+            pltpu.SemaphoreType.DMA((4,)),
         ]
 
     def __init__(self, place, object_ref, below, beside, corner, sent, came):
@@ -310,9 +314,17 @@
         self.below, self.beside, self.corner = below, beside, corner
         margin = corner.shape[1]
         self.margin = margin
-        self.from_below = remote(
-            object_ref.at[:, pl.ds(0, margin), :], below, sent.at[0], came.at[0], row=place.up
-        )
+        first, rest = pl.ds(0, margin), pl.ds(margin, below.shape[2] - margin)
+        self.from_below = [
+            remote(
+                object_ref.at[:, first, cols],
+                below.at[:, :, cols],
+                sent.at[at],
+                came.at[at],
+                row=place.up,
+            )
+            for at, cols in ((0, first), (3, rest))
+        ]
         self.from_beside = remote(
             object_ref.at[:, :, pl.ds(0, margin)], beside, sent.at[1], came.at[1], col=place.left
         )
@@ -321,8 +333,12 @@
         )
 
     def start(self):
-        pl.when(self.place.has_up)(self.from_below.start)
         pl.when(self.place.has_left)(self.from_beside.start)
+
+        @pl.when(self.place.has_up)
+        def _():
+            for copy in self.from_below:
+                copy.start()
 
     def finish(self, ext_ref):
         place, margin = self.place, self.margin
@@ -331,8 +347,9 @@
 
         @pl.when(place.has_down)
         def _():
-            self.from_below.wait_recv()
+            self.from_below[0].wait_recv()
             pl.when(place.has_left)(self.from_corner.start)
+            self.from_below[1].wait_recv()
             ext_ref[:, tile_rows:, :tile_cols] = self.below[...]
 
         @pl.when(jnp.logical_not(place.has_down))
@@ -355,7 +372,12 @@
 
     def settle(self):
         place = self.place
-        pl.when(place.has_up)(self.from_below.wait_send)
+
+        @pl.when(place.has_up)
+        def _():
+            for copy in self.from_below:
+                copy.wait_send()
+
         pl.when(place.has_left)(self.from_beside.wait_send)
         pl.when(jnp.logical_and(place.has_left, place.has_down))(self.from_corner.wait_send)
 
@@ -372,8 +394,8 @@
             pltpu.VMEM((2, margin, tile_cols), jnp.float32),
             pltpu.VMEM((2, margin, margin), jnp.float32),
             pltpu.VMEM((2, margin, margin), jnp.float32),
-            pltpu.SemaphoreType.DMA((6,)),
-            pltpu.SemaphoreType.DMA((6,)),
+            pltpu.SemaphoreType.DMA((8,)),
+            pltpu.SemaphoreType.DMA((8,)),
         ]
 
     def __init__(self, place, last, grad, total, left, right, above, below, over, under, sent, came):
@@ -383,15 +405,32 @@
         margin = over.shape[1]
         tile_rows, tile_cols = grad.shape[1] - margin, grad.shape[2] - margin
         self.sizes = margin, tile_rows, tile_cols
-        first, own = pl.ds(0, margin), pl.ds(0, tile_cols)
+        first = pl.ds(0, margin)
         self.to_right = remote(
             grad.at[:, :, pl.ds(tile_cols, margin)], left, sent.at[0], came.at[0], col=place.right
         )
         self.to_left = remote(grad.at[:, :, first], right, sent.at[1], came.at[1], col=place.left)
-        self.to_down = remote(
-            total.at[:, pl.ds(tile_rows, margin), own], above, sent.at[2], came.at[2], row=place.down
-        )
-        self.to_up = remote(total.at[:, first, own], below, sent.at[3], came.at[3], row=place.up)
+        rest = pl.ds(margin, tile_cols - margin)
+        self.to_down = [
+            remote(
+                total.at[:, pl.ds(tile_rows, margin), cols],
+                above.at[:, :, cols],
+                sent.at[at],
+                came.at[at],
+                row=place.down,
+            )
+            for at, cols in ((2, first), (6, rest))
+        ]
+        self.to_up = [
+            remote(
+                total.at[:, first, cols],
+                below.at[:, :, cols],
+                sent.at[at],
+                came.at[at],
+                row=place.up,
+            )
+            for at, cols in ((3, first), (7, rest))
+        ]
         self.pass_over = remote(
             above.at[:, :, first], over, sent.at[4], came.at[4], col=place.left
         )
@@ -421,22 +460,42 @@
                 self.to_left.wait_recv()
                 total[:, :, tile_cols:] += self.right[...]
 
-        pl.when(place.has_down)(self.to_down.start)
-        if not self.last:
-            pl.when(place.has_up)(self.to_up.start)
+        for half in range(2):
+            pl.when(place.has_down)(self.to_down[half].start)
+            if not self.last:
+                pl.when(place.has_up)(self.to_up[half].start)
+
+    def pass_on(self):
+        place = self.place
+        if self.last:
+            return
+
+        @pl.when(place.has_up)
+        def _():
+            self.to_down[0].wait_recv()
+            pl.when(place.has_left)(self.pass_over.start)
+
+        @pl.when(place.has_down)
+        def _():
+            self.to_up[0].wait_recv()
+            pl.when(place.has_left)(self.pass_under.start)
+
+    def update_inside(self, old_ref, new_ref, factor):
+        total = self.total
+        margin, tile_rows, tile_cols = self.sizes
+        new_ref[:, margin:tile_rows, :tile_cols] = (
+            old_ref[:, margin:tile_rows, :tile_cols] + factor * total[:, margin:tile_rows, :tile_cols]
+        )
 
     def finish(self, old_ref, new_ref, factor):
         place, total = self.place, self.total
         margin, tile_rows, tile_cols = self.sizes
-        new_ref[:, margin:tile_rows, :tile_cols] = (
-            old_ref[:, margin:tile_rows, :tile_cols] + factor * total[:, margin:tile_rows, :tile_cols]
-        )
 
         @pl.when(place.has_up)
         def _():
-            self.to_down.wait_recv()
-            if not self.last:
-                pl.when(place.has_left)(self.pass_over.start)
+            if self.last:
+                self.to_down[0].wait_recv()
+            self.to_down[1].wait_recv()
             new_ref[:, :margin, :tile_cols] = old_ref[:, :margin, :tile_cols] + factor * (
                 total[:, :margin, :tile_cols] + self.above[...]
             )
@@ -452,8 +511,7 @@
 
         @pl.when(place.has_down)
         def _():
-            self.to_up.wait_recv()
-            pl.when(place.has_left)(self.pass_under.start)
+            self.to_up[1].wait_recv()
             new_ref[:, tile_rows:, :tile_cols] = old_ref[:, tile_rows:, :tile_cols] + factor * (
                 total[:, tile_rows:, :tile_cols] + self.below[...]
             )
@@ -496,10 +554,12 @@
     def settle(self):
         place = self.place
         pl.when(place.has_right)(self.to_right.wait_send)
-        pl.when(place.has_down)(self.to_down.wait_send)
+        for half in range(2):
+            pl.when(place.has_down)(self.to_down[half].wait_send)
+            if not self.last:
+                pl.when(place.has_up)(self.to_up[half].wait_send)
         if not self.last:
             pl.when(place.has_left)(self.to_left.wait_send)
-            pl.when(place.has_up)(self.to_up.wait_send)
             pl.when(jnp.logical_and(place.has_left, place.has_up))(self.pass_over.wait_send)
             pl.when(jnp.logical_and(place.has_left, place.has_down))(self.pass_under.wait_send)
 
@@ -735,13 +795,17 @@
     for step in range(OUTER):
         last = step == OUTER - 1
         ext, probe = exts[step % 2], probes[step % 2]
-        power = pass_over_windows(
-            off_ref, cnt_ref, ext, probe, ordered, tab_ref, grad_ref, pgrad_ref, slabs, padded
-        )
         rim_refs, sum_refs = step_refs[2 * step : 2 * step + 2]
         rims = Rims(place, last, grad_ref, *rim_refs)
         sums = Sums(place, *sum_refs)
-        sums.fill(pgrad_ref, power)
+
+        def summed(power):
+            sums.fill(pgrad_ref, power)
+            sums.start()
+
+        pass_over_windows(
+            off_ref, cnt_ref, ext, probe, ordered, tab_ref, grad_ref, pgrad_ref, slabs, padded, summed
+        )
         if last:
             exchange(rims, sums, ext, probe, out_ref, new_ref)
         else:
@@ -751,16 +815,21 @@
 
 def exchange(rims, sums, ext_ref, probe_ref, out_ref, new_ref):
     window = probe_ref.shape[1]
-    sums.start()
     rims.start()
     sums.start_near()
+    if not rims.last:
+        rims.start_rows()
     sums.start_far()
-    rims.start_rows()
+    if rims.last:
+        rims.start_rows()
+    mean = jnp.sum(probe_ref[...] * probe_ref[...]) / (window * window)
+    factor = object_step / (mean + tiny_value)
     power = sums.start_back()
+    rims.update_inside(ext_ref, out_ref, factor)
     sums.start_back_near()
-    mean = jnp.sum(probe_ref[...] * probe_ref[...]) / (window * window)
-    rims.finish(ext_ref, out_ref, object_step / (mean + tiny_value))
+    rims.pass_on()
     sums.pass_on()
+    rims.finish(ext_ref, out_ref, factor)
     sums.finish(power, probe_ref, new_ref)
     rims.settle()
     sums.settle()

time: 71.8 us -> 71.9 us (level)
  the two profiles are of different devices: /device:TPU:25 before, /device:TPU:1 now
where the time goes in v4:
time: 71.9 us; the launch traced here: 71.7 us
  Pallas kernels  67.7 us (94%)
  local copies, waits for them, and re-layouts  2.72 us (4%)
  between operations  1.29 us (2%)
    pallas_call x1, Pallas kernels, shards_by_kernel(): pl.pallas_call(functools.partial(whole_kernel, [len(group) for group in g...  67.7 us
    unnamed x4, local copies, waits for them, and re-layouts  2.72 us

profile of v4, /device:TPU:1, one launch (start us, length us, event | category | flops | bytes accessed | tf_op | source)
XLA Modules:
  0.0 71.7 jit_solution(3653058564816817050)
XLA Ops:
  1.3 67.7 %refinement.1 = (f32[2,256,256]{2,1,0:T(8,128)}, f32[2,256,256]{2,1,0:T(8,128)}) custom-call(s32[1,1,2,2]{3,2,1,0:T(2,128)} %off_ref.1, s32[1,1]{1,0:T(1,128)S(6)} %copy.10.cnt_ref, f32[2,256,256]{2,1,0:T(8,128)} %object_hbm.1, f32[2,256,256]{2,1,0:T(8,128)} %probe_hbm.1, f32[2,256,256]{2,1,0:T(8,128)} %amp_hbm.1, bf16[9,256,256]{2,1,0:T(8,128)(2,1)} %constant.2.clone.tab_hbm), custom_call_target="tpu_custom_call" | custom-call | tf_op jit(solution)/shard_map/refinement/pallas_call | solution.py:863
  69.0 0.0 copy-start
  69.0 1.9 %copy.11 = f32[2,256,256]{2,1,0:T(8,128)} copy(f32[2,256,256]{2,1,0:T(8,128)} %get-tuple-element.4) | data formatting | bytes 1048576
  70.9 0.0 copy-done
  70.9 0.8 %copy.12 = f32[2,256,256]{2,1,0:T(8,128)} copy(f32[2,256,256]{2,1,0:T(8,128)S(1)} %copy-done) | data formatting | bytes 1048576
Async XLA Ops:
  69.0 1.9 %copy-start = (f32[2,256,256]{2,1,0:T(8,128)S(1)}, f32[2,256,256]{2,1,0:T(8,128)}, u32[]{:S(2)}) copy-start(f32[2,256,256]{2,1,0:T(8,128)} %get-tuple-element.5) | copy-start | bytes 1572868

commit v5 on v4

--- a/solution.py
+++ b/solution.py
@@ -590,7 +590,7 @@
             pltpu.VMEM((far, full, 128), jnp.float32),
             pltpu.VMEM((more_far, full, 128), jnp.float32),
             pltpu.VMEM((cols, near, far, deep, 128), jnp.float32),
-            pltpu.SemaphoreType.DMA((2, more_cols)),
+            pltpu.SemaphoreType.DMA((2, more_cols, near)),
             pltpu.SemaphoreType.DMA((2, 2, more_near)),
             pltpu.SemaphoreType.DMA((2, 2, more_far)),
             pltpu.SemaphoreType.DMA((2, more_cols, near)),
@@ -611,15 +611,19 @@
         def other_far(step):
             return lax.rem(self.at_far + step, far)
 
+        self.other_near = other_near
         self.over_cols = [
-            remote(
-                whole.at[place.other_col(step)],
-                from_cols.at[step - 1],
-                sems.at[0, step - 1],
-                sems.at[1, step - 1],
-                col=place.other_col(step),
-            )
-            for step in range(1, place.cols)
+            [
+                remote(
+                    whole.at[place.other_col(step), other_near(block)],
+                    from_cols.at[step - 1, other_near(block)],
+                    sems.at[0, step - 1, block],
+                    sems.at[1, step - 1, block],
+                    col=place.other_col(step),
+                )
+                for step in range(1, place.cols)
+            ]
+            for block in [*range(1, near), 0]
         ]
         self.over_near = [
             remote(
@@ -700,16 +704,20 @@
             self.whole[col, near, far, self.deep :] = folded
 
     def start(self):
-        for copy in self.over_cols:
-            copy.start()
+        for copies in self.over_cols:
+            for copy in copies:
+                copy.start()
 
     def start_near(self):
-        self.part[...] = self.whole[self.place.col]
-        for step, copy in enumerate(self.over_cols):
-            copy.wait_recv()
-            self.part[...] += self.from_cols[step]
-        for copy in self.over_near:
-            copy.start()
+        for block, copies in zip([*range(1, self.near), 0], self.over_cols):
+            at = self.other_near(block)
+            total = self.whole[self.place.col, at]
+            for step, copy in enumerate(copies):
+                copy.wait_recv()
+                total = total + self.from_cols[step, at]
+            self.part[at] = total
+            if block:
+                self.over_near[block - 1].start()
 
     def start_far(self):
         total = self.part[self.at_near]
@@ -756,8 +764,8 @@
         new_ref[...] = moved * jnp.sqrt(old / (new + tiny_value))
 
     def settle(self):
-        copies = self.over_cols + self.over_near + self.over_far + self.back_far + self.back_near
-        for copy in copies + sum(self.back_cols, []):
+        copies = self.over_near + self.over_far + self.back_far + self.back_near
+        for copy in copies + sum(self.over_cols + self.back_cols, []):
             copy.wait_send()
 
 
@@ -835,6 +843,30 @@
     sums.settle()
 
 
+def hand_over_kernel(object_ref, probe_ref, object_out, probe_out, sems):
+    copies = [
+        pltpu.make_async_copy(object_ref, object_out, sems.at[0]),
+        pltpu.make_async_copy(probe_ref, probe_out, sems.at[1]),
+    ]
+    for copy in copies:
+        copy.start()
+    for copy in copies:
+        copy.wait()
+
+
+def hand_over(*results):
+    anywhere = pl.BlockSpec(memory_space=pl.ANY)
+    return pl.pallas_call(
+        hand_over_kernel,
+        out_shape=tuple(jax.ShapeDtypeStruct(value.shape, value.dtype) for value in results),
+        in_specs=[anywhere] * 2,
+        out_specs=(anywhere, anywhere),
+        scratch_shapes=[pltpu.SemaphoreType.DMA((2,))],
+        compiler_params=pltpu.CompilerParams(vmem_limit_bytes=60 * 2**20),
+        name="hand_over",
+    )(*results)
+
+
 def shards_by_kernel(object_field, probe_field, amplitudes, offsets, counts):
     tables = jnp.asarray(make_tables(probe_field.shape[1]))
     _, tile_rows, tile_cols = object_field.shape
@@ -860,7 +892,7 @@
     smem = pl.BlockSpec(memory_space=pltpu.SMEM)
     vmem = pl.BlockSpec(memory_space=pltpu.VMEM)
     anywhere = pl.BlockSpec(memory_space=pl.ANY)
-    return pl.pallas_call(
+    results = pl.pallas_call(
         functools.partial(whole_kernel, [len(group) for group in groups]),
         out_shape=(
             jax.ShapeDtypeStruct(object_field.shape, jnp.float32),
@@ -874,6 +906,7 @@
         ),
         name="refinement",
     )(offsets, counts, object_field, probe_field, amplitudes, tables)
+    return hand_over(*results)
 
 
 def shards(object_field, probe_field, amplitudes, offsets, counts):

time: 71.9 us -> 102 us (1.42)
  the two profiles are of different devices: /device:TPU:1 before, /device:TPU:25 now
where the time goes in v5:
time: 102 us; the launch traced here: 100 us
  Pallas kernels  98.8 us (97%)
  between operations  1.29 us (1%)
    pallas_call x1, Pallas kernels, shards_by_kernel(): pl.pallas_call(functools.partial(whole_kernel, [len(group) for group in g...  65.9 us
    pallas_call x1, Pallas kernels, hand_over(): pl.pallas_call(hand_over_kernel, out_shape=tuple((jax.ShapeDtypeStruct(va...  32.9 us

profile of v5, /device:TPU:25, one launch (start us, length us, event | category | flops | bytes accessed | tf_op | source)
XLA Modules:
  0.0 100.1 jit_solution(1729039654616208051)
XLA Ops:
  1.3 65.9 %refinement.1 = (f32[2,256,256]{2,1,0:T(8,128)}, f32[2,256,256]{2,1,0:T(8,128)}) custom-call(s32[1,1,2,2]{3,2,1,0:T(2,128)} %off_ref.1, s32[1,1]{1,0:T(1,128)S(6)} %copy.8.cnt_ref, f32[2,256,256]{2,1,0:T(8,128)} %object_hbm.1, f32[2,256,256]{2,1,0:T(8,128)} %probe_hbm.1, f32[2,256,256]{2,1,0:T(8,128)} %amp_hbm.1, bf16[9,256,256]{2,1,0:T(8,128)(2,1)} %constant.2.clone.tab_hbm), custom_call_target="tpu_custom_call" | custom-call | tf_op jit(solution)/shard_map/refinement/pallas_call | solution.py:895
  67.2 32.9 %hand_over.1 = (f32[2,256,256]{2,1,0:T(8,128)}, f32[2,256,256]{2,1,0:T(8,128)}) custom-call(f32[2,256,256]{2,1,0:T(8,128)} %get-tuple-element.4.object_ref, f32[2,256,256]{2,1,0:T(8,128)} %get-tuple-element.5.probe_ref), custom_call_target="tpu_custom_call" | custom-call | tf_op jit(solution)/shard_map/hand_over/pallas_call | solution.py:859
